TPU v7x, 32 devices: a whole 2x2x4 slice. The times are simulated.
32 devices in a mesh: fsdp: 4 (over y, x), ctx: 8 (over z, core).
Axes of the slice: x: 2, y: 2, z: 4, core: 2. Of those that a mesh axis runs over, the one named last changes fastest.
Arguments:
- tokens: bfloat16 [4, 1024, 960], P('fsdp', 'ctx'), may hold values from -6 to 6
- positions: int32 [4, 1024], P('fsdp', 'ctx'), may hold values from 0 to 1023, as said below
- cotangent: bfloat16 [4, 1024, 960], P('fsdp', 'ctx'), may hold values from -6 to 6
- w_query: bfloat16 [2, 960, 960], P(None, 'fsdp'), may hold values from -0.1875 to 0.1875
- w_key: bfloat16 [2, 960, 320], P(None, 'fsdp'), may hold values from -0.1875 to 0.1875
- w_value: bfloat16 [2, 960, 320], P(None, 'fsdp'), may hold values from -0.1875 to 0.1875
- w_out: bfloat16 [2, 960, 960], P(None, 'fsdp'), may hold values from -1 to 1
- w_gate: bfloat16 [2, 960, 2560], P(None, 'fsdp'), may hold values from -0.1875 to 0.1875
- w_up: bfloat16 [2, 960, 2560], P(None, 'fsdp'), may hold values from -0.1875 to 0.1875
- w_down: bfloat16 [2, 2560, 960], P(None, 'fsdp'), may hold values from -0.125 to 0.125
- gain_attn: bfloat16 [2, 960], P(None, 'fsdp'), may hold values from 0.5 to 1.5
- gain_mlp: bfloat16 [2, 960], P(None, 'fsdp'), may hold values from 0.5 to 1.5
Outputs:
- output: bfloat16 [4, 1024, 960], P('fsdp', 'ctx')
- grad_tokens: bfloat16 [4, 1024, 960], P('fsdp', 'ctx')
- grad_query: float32 [2, 960, 960], P(None, 'fsdp')
- grad_key: float32 [2, 960, 320], P(None, 'fsdp')
- grad_value: float32 [2, 960, 320], P(None, 'fsdp')
- grad_out: float32 [2, 960, 960], P(None, 'fsdp')
- grad_gate: float32 [2, 960, 2560], P(None, 'fsdp')
- grad_up: float32 [2, 960, 2560], P(None, 'fsdp')
- grad_down: float32 [2, 2560, 960], P(None, 'fsdp')
- grad_gain_attn: float32 [2, 960], P(None, 'fsdp')
- grad_gain_mlp: float32 [2, 960], P(None, 'fsdp')
Inputs may be any that keep to these rules, and one draw needn't show every extreme that they name: Row s lists the positions of sequence s in the order of its tokens: a permutation of 0 to 1023 made of whole blocks of 64 consecutive positions in ascending order; the 128 tokens of one index of ctx are block b followed by block 15 - b.
All inputs are finite; a program needn't handle non-finite values.
Results may differ from a plain program's by a relative error of at most 0.03.
Values may be sent and summed in bfloat16 or wider, within the bound.
A program may use at most 384 MiB of HBM per device.

v0:
```python
import math

import jax
import jax.numpy as jnp
from jax import lax
from jax.sharding import PartitionSpec as P

QUERY_HEADS = 15
KEY_VALUE_HEADS = 5
HEAD_SIZE = 64


EPS = 1e-05
ROPE_BASE = 100000.0
SCORE_FLOOR = -1e30


def rope_tables(token_positions):
    half = HEAD_SIZE // 2
    freqs = ROPE_BASE ** (-jnp.arange(half, dtype=jnp.float32) * 2.0 / HEAD_SIZE)
    angles = token_positions.astype(jnp.float32)[:, None] * freqs[None, :]
    return (jnp.cos(angles)[:, None, :], jnp.sin(angles)[:, None, :])


def apply_rotary(value_rows, cosine_table, sine_table):
    half = HEAD_SIZE // 2
    first = value_rows[..., :half]
    second = value_rows[..., half:]
    return jnp.concatenate(
        [first * cosine_table - second * sine_table, second * cosine_table + first * sine_table],
        axis=-1,
    )


def rotary_backward(grads, cosine_table, sine_table):
    half = HEAD_SIZE // 2
    first = grads[..., :half]
    second = grads[..., half:]
    return jnp.concatenate(
        [first * cosine_table + second * sine_table, second * cosine_table - first * sine_table],
        axis=-1,
    )


def rms_factor(hidden):
    return lax.rsqrt(jnp.mean(hidden * hidden, axis=-1, keepdims=True) + EPS)


def norm_back(hidden, gain, grad_out):
    factor = rms_factor(hidden)
    scaled = grad_out * gain
    grad_gain = jnp.sum(grad_out * hidden * factor, axis=0)
    inner = jnp.mean(hidden * scaled, axis=-1, keepdims=True)
    return (factor * scaled - hidden * (factor * factor * factor) * inner, grad_gain)


def transpose_matmul(left, right):
    return lax.dot_general(
        left, right, (((1,), (1,)), ((), ())), preferred_element_type=jnp.float32
    )


def transpose_by(left, right):
    return lax.dot_general(
        left, right, (((0,), (0,)), ((), ())), preferred_element_type=jnp.float32
    )


def split_pairs(block_attention):
    block_count = block_attention.shape[0]
    key_rows = block_attention[:, : KEY_VALUE_HEADS * HEAD_SIZE].reshape(
        block_count, KEY_VALUE_HEADS, HEAD_SIZE
    )
    value_rows = block_attention[:, KEY_VALUE_HEADS * HEAD_SIZE :].reshape(
        block_count, KEY_VALUE_HEADS, HEAD_SIZE
    )
    return (key_rows, value_rows)


def block_scores(query_rows, key_rows, query_places, key_places, score_scale):
    scores = (
        jnp.einsum("qkgd,skd->kgqs", query_rows, key_rows, preferred_element_type=jnp.float32)
        * score_scale
    )
    visible = key_places[None, :] <= query_places[:, None]
    return (jnp.where(visible, scores, SCORE_FLOOR), visible)


def make_fold(query_rows, query_places, score_scale):

    def fold_keys(carry, piece, start):
        block_attention, key_places = piece
        block_count = block_attention.shape[0]
        model_width = math.gcd(block_count, 512)

        def fold_one_step(state, item):
            sub_block, sub_places = item
            top, total, running_totals = state
            key_rows, value_rows = split_pairs(sub_block)
            scores, visible = block_scores(
                query_rows, key_rows, query_places, sub_places, score_scale
            )
            new_top = jnp.maximum(top, jnp.max(scores, axis=-1))
            weights = jnp.where(visible, jnp.exp(scores - new_top[..., None]), 0.0)
            factor = jnp.exp(top - new_top)
            total = total * factor + jnp.sum(weights, axis=-1)
            running_totals = running_totals * factor[..., None] + jnp.einsum(
                "kgqs,skd->kgqd",
                weights.astype(jnp.bfloat16),
                value_rows,
                preferred_element_type=jnp.float32,
            )
            return ((new_top, total, running_totals), None)

        items = (
            block_attention.reshape(
                block_count // model_width, model_width, block_attention.shape[1]
            ),
            key_places.reshape(block_count // model_width, model_width),
        )
        carry, unused = lax.scan(fold_one_step, carry, items)
        return carry

    return fold_keys


def key_grads(
    query_rows,
    mixed_gradient,
    delta,
    top,
    total,
    query_places,
    every_pair,
    every_place,
    score_scale,
):
    block_count = every_pair.shape[0]
    model_width = math.gcd(block_count, 512)
    log_total = top + jnp.log(total)

    def key_one_step(running_totals, item):
        sub_block, sub_places = item
        key_rows, value_rows = split_pairs(sub_block)
        scores, visible = block_scores(query_rows, key_rows, query_places, sub_places, score_scale)
        probs = jnp.where(visible, jnp.exp(scores - log_total[..., None]), 0.0)
        values_gradient = jnp.einsum(
            "kgqs,qkgd->skd",
            probs.astype(jnp.bfloat16),
            mixed_gradient,
            preferred_element_type=jnp.float32,
        )
        grad_probs = jnp.einsum(
            "qkgd,skd->kgqs", mixed_gradient, value_rows, preferred_element_type=jnp.float32
        )
        grad_scores = (probs * (grad_probs - delta[..., None])).astype(jnp.bfloat16)
        running_totals = running_totals + jnp.einsum(
            "kgqs,skd->kgqd", grad_scores, key_rows, preferred_element_type=jnp.float32
        )
        keys_gradient = (
            jnp.einsum(
                "kgqs,qkgd->skd", grad_scores, query_rows, preferred_element_type=jnp.float32
            )
            * score_scale
        )
        joined = jnp.concatenate(
            [
                keys_gradient.reshape(model_width, KEY_VALUE_HEADS * HEAD_SIZE),
                values_gradient.reshape(model_width, KEY_VALUE_HEADS * HEAD_SIZE),
            ],
            axis=1,
        )
        return (running_totals, joined)

    items = (
        every_pair.reshape(block_count // model_width, model_width, every_pair.shape[1]),
        every_place.reshape(block_count // model_width, model_width),
    )
    initial_totals = jnp.zeros(
        (KEY_VALUE_HEADS, QUERY_HEADS // KEY_VALUE_HEADS, query_rows.shape[0], HEAD_SIZE),
        jnp.float32,
    )
    running_totals, sequence_pieces = lax.scan(key_one_step, initial_totals, items)
    return (
        running_totals * score_scale,
        sequence_pieces.reshape(block_count, 2 * KEY_VALUE_HEADS * HEAD_SIZE),
    )


def reduce_grads(gradients):
    parts = lax.axis_size("fsdp")
    packed = jnp.concatenate([item.reshape(parts, -1) for item in gradients], axis=1)
    length = packed.shape[1]
    mine = lax.psum_scatter(
        packed.astype(jnp.bfloat16), "fsdp", scatter_dimension=0, tiled=True
    ).astype(jnp.float32)
    mine = lax.psum(mine.astype(jnp.bfloat16), "ctx").astype(jnp.float32).reshape(length)
    results = []
    offset = 0
    for item in gradients:
        amount = item.size // parts
        results.append(
            mine[offset : offset + amount].reshape((item.shape[0] // parts,) + item.shape[1:])
        )
        offset = offset + amount
    return results


def on_device(
    tokens,
    positions,
    cotangent,
    w_query,
    w_key,
    w_value,
    w_out,
    w_gate,
    w_up,
    w_down,
    gain_attn,
    gain_mlp,
):
    layers = w_query.shape[0]
    token_positions = positions[0]
    token_rows = token_positions.shape[0]
    query_groups = QUERY_HEADS // KEY_VALUE_HEADS
    score_scale = HEAD_SIZE ** (-0.5)
    cosine_table, sine_table = rope_tables(token_positions)
    hidden = tokens[0].astype(jnp.float32)
    saved = []
    for index in range(layers):
        weights = (
            lax.all_gather(w_query[index], "fsdp", axis=0, tiled=True),
            lax.all_gather(w_key[index], "fsdp", axis=0, tiled=True),
            lax.all_gather(w_value[index], "fsdp", axis=0, tiled=True),
            lax.all_gather(w_out[index], "fsdp", axis=0, tiled=True),
            lax.all_gather(w_gate[index], "fsdp", axis=0, tiled=True),
            lax.all_gather(w_up[index], "fsdp", axis=0, tiled=True),
            lax.all_gather(w_down[index], "fsdp", axis=0, tiled=True),
            lax.all_gather(gain_attn[index], "fsdp", axis=0, tiled=True),
            lax.all_gather(gain_mlp[index], "fsdp", axis=0, tiled=True),
        )
        query_w, key_matrix, value_w, output_matrix, gate_w, up_w, down_w, attn_gain, mlp_gain = (
            weights
        )
        normalized_rows = (hidden * rms_factor(hidden) * attn_gain).astype(jnp.bfloat16)
        query_rows = apply_rotary(
            jnp.dot(normalized_rows, query_w, preferred_element_type=jnp.float32).reshape(
                token_rows, QUERY_HEADS, HEAD_SIZE
            ),
            cosine_table,
            sine_table,
        )
        query_rows = query_rows.astype(jnp.bfloat16).reshape(
            token_rows, KEY_VALUE_HEADS, query_groups, HEAD_SIZE
        )
        key_rows = apply_rotary(
            jnp.dot(normalized_rows, key_matrix, preferred_element_type=jnp.float32).reshape(
                token_rows, KEY_VALUE_HEADS, HEAD_SIZE
            ),
            cosine_table,
            sine_table,
        )
        key_rows = key_rows.astype(jnp.bfloat16)
        value_rows = jnp.dot(normalized_rows, value_w, preferred_element_type=jnp.float32).astype(
            jnp.bfloat16
        )
        block_pairs = jnp.concatenate(
            [key_rows.reshape(token_rows, KEY_VALUE_HEADS * HEAD_SIZE), value_rows], axis=1
        )
        start_state = (
            jnp.full((KEY_VALUE_HEADS, query_groups, token_rows), SCORE_FLOOR, jnp.float32),
            jnp.zeros((KEY_VALUE_HEADS, query_groups, token_rows), jnp.float32),
            jnp.zeros((KEY_VALUE_HEADS, query_groups, token_rows, HEAD_SIZE), jnp.float32),
        )
        fold_keys = make_fold(query_rows, token_positions, score_scale)
        top, total, running_totals = fold_keys(
            start_state,
            (
                lax.all_gather(block_pairs, "ctx", axis=0, tiled=True),
                lax.all_gather(token_positions, "ctx", axis=0, tiled=True),
            ),
            jnp.int32(0),
        )
        extra = (block_pairs,)
        mixed_heads = jnp.transpose(running_totals / total[..., None], (2, 0, 1, 3)).reshape(
            token_rows, QUERY_HEADS * HEAD_SIZE
        )
        mixed_low = mixed_heads.astype(jnp.bfloat16)
        middle = hidden + jnp.dot(mixed_low, output_matrix, preferred_element_type=jnp.float32)
        normed_mlp = (middle * rms_factor(middle) * mlp_gain).astype(jnp.bfloat16)
        gate = jnp.dot(normed_mlp, gate_w, preferred_element_type=jnp.float32)
        upward = jnp.dot(normed_mlp, up_w, preferred_element_type=jnp.float32)
        inner = (jax.nn.silu(gate) * upward).astype(jnp.bfloat16)
        saved.append(
            (
                hidden,
                normalized_rows,
                query_rows,
                mixed_heads,
                mixed_low,
                top,
                total,
                middle,
                normed_mlp,
                gate,
                upward,
                inner,
                extra,
            )
        )
        hidden = middle + jnp.dot(inner, down_w, preferred_element_type=jnp.float32)
    output = hidden.astype(jnp.bfloat16)[None]
    grad = cotangent[0].astype(jnp.float32)
    collected = [None] * layers
    for index in reversed(range(layers)):
        (
            hidden,
            normalized_rows,
            query_rows,
            mixed_heads,
            mixed_low,
            top,
            total,
            middle,
            normed_mlp,
            gate,
            upward,
            inner,
            extra,
        ) = saved[index]
        weights = (
            lax.all_gather(w_query[index], "fsdp", axis=0, tiled=True),
            lax.all_gather(w_key[index], "fsdp", axis=0, tiled=True),
            lax.all_gather(w_value[index], "fsdp", axis=0, tiled=True),
            lax.all_gather(w_out[index], "fsdp", axis=0, tiled=True),
            lax.all_gather(w_gate[index], "fsdp", axis=0, tiled=True),
            lax.all_gather(w_up[index], "fsdp", axis=0, tiled=True),
            lax.all_gather(w_down[index], "fsdp", axis=0, tiled=True),
            lax.all_gather(gain_attn[index], "fsdp", axis=0, tiled=True),
            lax.all_gather(gain_mlp[index], "fsdp", axis=0, tiled=True),
        )
        every_pair, every_place = (
            lax.all_gather(extra[0], "ctx", axis=0, tiled=True),
            lax.all_gather(token_positions, "ctx", axis=0, tiled=True),
        )
        query_w, key_matrix, value_w, output_matrix, gate_w, up_w, down_w, attn_gain, mlp_gain = (
            weights
        )
        grad_low = grad.astype(jnp.bfloat16)
        grad_down_w = transpose_by(inner, grad_low)
        grad_inner = transpose_matmul(grad_low, down_w)
        sigma = jax.nn.sigmoid(gate)
        grad_upward = (grad_inner * gate * sigma).astype(jnp.bfloat16)
        grad_gating = (grad_inner * upward * sigma * (1.0 + gate * (1.0 - sigma))).astype(
            jnp.bfloat16
        )
        grad_gate_w = transpose_by(normed_mlp, grad_gating)
        grad_up_w = transpose_by(normed_mlp, grad_upward)
        grad_normed_mlp = transpose_matmul(grad_gating, gate_w) + transpose_matmul(
            grad_upward, up_w
        )
        grad_middle, grad_mlp_gain = norm_back(middle, mlp_gain, grad_normed_mlp)
        grad_middle = grad_middle + grad
        lower_branch = grad_middle.astype(jnp.bfloat16)
        grad_out_w = transpose_by(mixed_low, lower_branch)
        mixed_gradient = (
            transpose_matmul(lower_branch, output_matrix)
            .astype(jnp.bfloat16)
            .reshape(token_rows, KEY_VALUE_HEADS, query_groups, HEAD_SIZE)
        )
        delta = jnp.einsum(
            "icun,icun->cui",
            mixed_gradient.astype(jnp.float32),
            mixed_heads.reshape(token_rows, KEY_VALUE_HEADS, query_groups, HEAD_SIZE),
        )
        grad_queries, pair_terms = key_grads(
            query_rows,
            mixed_gradient,
            delta,
            top,
            total,
            token_positions,
            every_pair,
            every_place,
            score_scale,
        )
        diagonal_terms = lax.psum_scatter(
            pair_terms.astype(jnp.bfloat16), "ctx", scatter_dimension=0, tiled=True
        ).astype(jnp.float32)
        query_grad = jnp.transpose(grad_queries, (2, 0, 1, 3)).reshape(
            token_rows, QUERY_HEADS, HEAD_SIZE
        )
        query_grad = (
            rotary_backward(query_grad, cosine_table, sine_table)
            .reshape(token_rows, QUERY_HEADS * HEAD_SIZE)
            .astype(jnp.bfloat16)
        )
        key_gradient_part = rotary_backward(
            diagonal_terms[:, : KEY_VALUE_HEADS * HEAD_SIZE].reshape(
                token_rows, KEY_VALUE_HEADS, HEAD_SIZE
            ),
            cosine_table,
            sine_table,
        )
        key_gradient_part = key_gradient_part.reshape(
            token_rows, KEY_VALUE_HEADS * HEAD_SIZE
        ).astype(jnp.bfloat16)
        value_gradient_part = diagonal_terms[:, KEY_VALUE_HEADS * HEAD_SIZE :].astype(jnp.bfloat16)
        grad_query_w = transpose_by(normalized_rows, query_grad)
        grad_key_w = transpose_by(normalized_rows, key_gradient_part)
        grad_value_w = transpose_by(normalized_rows, value_gradient_part)
        grad_normed = (
            transpose_matmul(query_grad, query_w)
            + transpose_matmul(key_gradient_part, key_matrix)
            + transpose_matmul(value_gradient_part, value_w)
        )
        grad_hidden, grad_attn_gain = norm_back(hidden, attn_gain, grad_normed)
        grad = grad_hidden + grad_middle
        collected[index] = reduce_grads(
            (
                grad_query_w,
                grad_key_w,
                grad_value_w,
                grad_out_w,
                grad_gate_w,
                grad_up_w,
                grad_down_w,
                grad_attn_gain,
                grad_mlp_gain,
            )
        )
    grad_tokens = grad.astype(jnp.bfloat16)[None]
    stacked = [
        jnp.stack([collected[index][member] for index in range(layers)]) for member in range(9)
    ]
    return (
        output,
        grad_tokens,
        stacked[0],
        stacked[1],
        stacked[2],
        stacked[3],
        stacked[4],
        stacked[5],
        stacked[6],
        stacked[7],
        stacked[8],
    )


def solution(mesh):
    placed = (
        P("fsdp", "ctx", None),
        P("fsdp", "ctx"),
        P("fsdp", "ctx", None),
        P(None, "fsdp", None),
        P(None, "fsdp", None),
        P(None, "fsdp", None),
        P(None, "fsdp", None),
        P(None, "fsdp", None),
        P(None, "fsdp", None),
        P(None, "fsdp", None),
        P(None, "fsdp"),
        P(None, "fsdp"),
    )
    return jax.shard_map(
        on_device,
        mesh=mesh,
        in_specs=placed,
        out_specs=(
            P("fsdp", "ctx", None),
            P("fsdp", "ctx", None),
            P(None, "fsdp", None),
            P(None, "fsdp", None),
            P(None, "fsdp", None),
            P(None, "fsdp", None),
            P(None, "fsdp", None),
            P(None, "fsdp", None),
            P(None, "fsdp", None),
            P(None, "fsdp"),
            P(None, "fsdp"),
        ),
        check_vma=False,
    )
```

profile of v0, /device:TPU:0, one launch (start us, length us, event | category | flops | bytes accessed | tf_op | source)
XLA Modules:
  0.0 2196.1 jit_solution(12674632206172376997)
XLA Ops:
  14.0 11.5 all-reduce.7
  29.0 14.9 all-gather.2
  46.3 15.8 all-gather.3
  81.4 11.9 all-gather
  96.1 21.5 all-gather.12
  120.9 22.9 %all-gather.11 = bf16[1,960,320]{2,0,1:T(2,128)(2,1)S(1)} all-gather(bf16[1,240,320]{2,0,1:T(2,128)(2,1)S(1)} %copy.245), channel_id=13, replica_groups=mesh['fsdp'=4,'ctx'=8] {'fsdp'}, dimensions={1}, use_global_device_ids=true | all-gather | bytes 768000 | tf_op jit(solution)/shard_map/all_gather | solution.py:234
  161.5 16.3 all-gather.38.cloned.1.call-done
  180.5 58.3 %all-gather.40.cloned.1.call-done = bf16[1,960,2560]{2,1,0:T(8,128)(2,1)} async-done(((bf16[1,240,2560]{2,1,0:T(8,128)(2,1)}), bf16[1,960,2560]{2,1,0:T(8,128)(2,1)}) %all-gather.40.cloned.1.call-update) | async-done | bytes 4915216 | tf_op jit(solution)/shard_map/all_gather | solution.py:237
  243.2 56.7 %all-gather.42.cloned.1.call-done = bf16[1,960,2560]{2,1,0:T(8,128)(2,1)} async-done(((bf16[1,240,2560]{2,1,0:T(8,128)(2,1)}), bf16[1,960,2560]{2,1,0:T(8,128)(2,1)}) %all-gather.42.cloned.1.call-update) | async-done | bytes 4915216 | tf_op jit(solution)/shard_map/all_gather | solution.py:238
  304.7 55.6 %all-gather.44.cloned.1.call-done = bf16[1,2560,960]{1,2,0:T(8,128)(2,1)} async-done(((bf16[1,640,960]{1,2,0:T(8,128)(2,1)}), bf16[1,2560,960]{1,2,0:T(8,128)(2,1)}) %all-gather.44.cloned.1.call-update) | async-done | bytes 4915216 | tf_op jit(solution)/shard_map/all_gather | solution.py:239
  368.4 28.0 %all-gather.46.cloned.1.call-done = bf16[1,960,960]{2,1,0:T(8,128)(2,1)} async-done(((bf16[1,240,960]{2,1,0:T(8,128)(2,1)}), bf16[1,960,960]{2,1,0:T(8,128)(2,1)}) %all-gather.46.cloned.1.call-update) | async-done | bytes 1843216 | tf_op jit(solution)/shard_map/all_gather | solution.py:233
  399.0 58.0 %all-gather.54.cloned.1.call-done = bf16[1,2560,960]{1,2,0:T(8,128)(2,1)} async-done(((bf16[1,640,960]{1,2,0:T(8,128)(2,1)}), bf16[1,2560,960]{1,2,0:T(8,128)(2,1)}) %all-gather.54.cloned.1.call-update) | async-done | bytes 4915216 | tf_op jit(solution)/shard_map/all_gather | solution.py:239
  461.3 23.7 %all-gather.34.cloned.1.call-done = bf16[1024,640]{0,1:T(8,128)(2,1)} async-done(((bf16[128,640]{0,1:T(8,128)(2,1)}), bf16[1024,640]{0,1:T(8,128)(2,1)}) %all-gather.34.cloned.1.call-update) | async-done | bytes 1310736 | tf_op jit(solution)/shard_map/all_gather | solution.py:280
  487.5 10.2 while.57
  498.8 20.7 all-gather.48.cloned.1.call-done
  522.2 58.5 %all-gather.52.cloned.1.call-done = bf16[1,960,2560]{2,1,0:T(8,128)(2,1)} async-done(((bf16[1,240,2560]{2,1,0:T(8,128)(2,1)}), bf16[1,960,2560]{2,1,0:T(8,128)(2,1)}) %all-gather.52.cloned.1.call-update) | async-done | bytes 4915216 | tf_op jit(solution)/shard_map/all_gather | solution.py:238
  585.0 56.7 %all-gather.50.cloned.1.call-done = bf16[1,960,2560]{2,1,0:T(8,128)(2,1)} async-done(((bf16[1,240,2560]{2,1,0:T(8,128)(2,1)}), bf16[1,960,2560]{2,1,0:T(8,128)(2,1)}) %all-gather.50.cloned.1.call-update) | async-done | bytes 4915216 | tf_op jit(solution)/shard_map/all_gather | solution.py:237
  655.6 21.0 while.58
  713.8 10.7 reshape.680
  735.8 8.5 reshape.491
  783.7 16.2 while.59
  853.9 10.9 reshape.686
  874.9 8.5 reshape.482
  887.1 8.5 reshape.483
  942.3 674.7 %all-reduce.14.cloned.1.call-done = (bf16[4,2458080]{1,0:T(4,128)(2,1)}, bf16[4,2458080]{1,0:T(4,128)(2,1)}) async-done(((bf16[4,2458080]{1,0:T(4,128)(2,1)}, bf16[4,2458080]{1,0:T(4,128)(2,1)}), (bf16[4,2458080]{1,0:T(4,128)(2,1)}, bf16[4,2458080]{1,0:T(4,128)(2,1)})) %all-reduce.14.cloned.1.call-update) | async-done | bytes 39329296
  1617.0 13.7 constant_dynamic-slice_fusion.4
  1632.8 12.1 constant_dynamic-slice_fusion.5
  1651.6 385.1 %all-reduce.12.cloned.1.call-done = (bf16[1,2458080]{1,0:T(2,128)(2,1)}, bf16[1,2458080]{1,0:T(2,128)(2,1)}) async-done(((bf16[1,2458080]{1,0:T(2,128)(2,1)}, bf16[1,2458080]{1,0:T(2,128)(2,1)}), (bf16[1,2458080]{1,0:T(2,128)(2,1)}, bf16[1,2458080]{1,0:T(2,128)(2,1)})) %all-reduce.12.cloned.1.call-update) | async-done | bytes 9832336 | tf_op jit(solution)/shard_map/psum | solution.py:197
  2036.7 11.7 convert_element_type.259
  2049.8 11.7 convert_element_type.258
  2065.5 11.8 slice_reduce_fusion.6
  2077.3 54.0 %slice_reduce_fusion = (f32[614400]{0:T(1024)}, f32[614400]{0:T(1024)}, f32[614400]{0:T(1024)}, f32[614400]{0:T(1024)}, f32[614400]{0:T(1024)}, /*index=5*/f32[614400]{0:T(1024)}) fusion(f32[1,2458080]{1,0:T(1,128)S(1)} %convert_element_type.259, f32[1,2458080]{1,0:T(1,128)S(1)} %convert_element_type.258), kind=kLoop, calls=%fused_computation.113 | loop fusion | bytes 29491200 | tf_op jit(solution)/shard_map/slice | solution.py:203
  (513 shorter events, 432.4 us)
Async XLA Ops:
  7.2 140.1 %all-gather.32.cloned.1.call-start = ((), (), s32[]{:S(2)}) async-start(), calls=%async_computation.2 | async-start | bytes 1474560 | tf_op jit(solution)/shard_map/all_gather | solution.py:280
  9.6 143.0 %copy-start.73 = (f32[128]{0:T(128)}, f32[128]{0:T(128)S(1)}, u32[]{:S(2)}) copy-start(f32[128]{0:T(128)S(1)} %get-tuple-element.772) | copy-start | bytes 1540
  25.5 127.1 %copy-start.70 = (f32[960]{0:T(1024)}, f32[960]{0:T(1024)S(1)}, u32[]{:S(2)}) copy-start(f32[960]{0:T(1024)S(1)} %convert_element_type.266) | copy-start | bytes 11524
  29.0 35.5 %copy-start = (bf16[1,128,960]{1,2,0:T(8,128)(2,1)S(1)}, bf16[1,128,960]{1,2,0:T(8,128)(2,1)}, u32[]{:S(2)}) copy-start(bf16[1,128,960]{1,2,0:T(8,128)(2,1)} %param.20) | copy-start | bytes 737284
  46.3 22.3 %copy-start.34 = (bf16[1,960,320]{1,2,0:T(8,128)(2,1)}, bf16[1,960,320]{1,2,0:T(8,128)(2,1)S(1)}, u32[]{:S(2)}) copy-start(bf16[1,960,320]{1,2,0:T(8,128)(2,1)S(1)} %copy.176) | copy-start | bytes 1843204
  66.4 82.3 %all-gather.36.cloned.1.call-start = ((), (), s32[]{:S(2)}) async-start(), calls=%async_computation.4 | async-start | bytes 2457600 | tf_op jit(solution)/shard_map/all_gather | solution.py:233
  68.6 109.2 %all-gather.38.cloned.1.call-start = ((), (), s32[]{:S(2)}) async-start(), calls=%async_computation.5 | async-start | bytes 2457600 | tf_op jit(solution)/shard_map/all_gather | solution.py:236
  69.7 169.1 %all-gather.40.cloned.1.call-start = ((), (), s32[]{:S(2)}) async-start(), calls=%async_computation.6 | async-start | bytes 6144000 | tf_op jit(solution)/shard_map/all_gather | solution.py:237
  73.1 226.8 %all-gather.42.cloned.1.call-start = ((), (), s32[]{:S(2)}) async-start(), calls=%async_computation.7 | async-start | bytes 6144000 | tf_op jit(solution)/shard_map/all_gather | solution.py:238
  76.5 283.8 %all-gather.44.cloned.1.call-start = ((), (), s32[]{:S(2)}) async-start(), calls=%async_computation.8 | async-start | bytes 6144000 | tf_op jit(solution)/shard_map/all_gather | solution.py:239
  79.8 316.5 %all-gather.46.cloned.1.call-start = ((), (), s32[]{:S(2)}) async-start(), calls=%async_computation.9 | async-start | bytes 2457600 | tf_op jit(solution)/shard_map/all_gather | solution.py:233
  80.6 376.4 %all-gather.54.cloned.1.call-start = ((), (), s32[]{:S(2)}) async-start(), calls=%async_computation.13 | async-start | bytes 6144000 | tf_op jit(solution)/shard_map/all_gather | solution.py:239
  81.3 403.7 %all-gather.34.cloned.1.call-start = ((), (), s32[]{:S(2)}) async-start(), calls=%async_computation.3 | async-start | bytes 1474560 | tf_op jit(solution)/shard_map/all_gather | solution.py:280
  161.4 16.4 copy-start.63
  161.5 81.7 %copy-start.57 = (bf16[128,5,3,64]{0,3,2,1:T(8,128)(2,1)}, bf16[128,5,3,64]{0,3,2,1:T(8,128)(2,1)S(1)}, u32[]{:S(2)}) copy-start(bf16[128,5,3,64]{0,3,2,1:T(8,128)(2,1)S(1)} %bitcast_convert_fusion.1) | copy-start | bytes 737284
  180.3 180.0 %copy-start.8 = (f32[128,960]{0,1:T(8,128)}, f32[128,960]{0,1:T(8,128)S(1)}, u32[]{:S(2)}) copy-start(f32[128,960]{0,1:T(8,128)S(1)} %get-tuple-element.780) | copy-start | bytes 1474564
  180.5 124.2 %copy-start.10 = (bf16[128,960]{0,1:T(8,128)(2,1)}, bf16[128,960]{0,1:T(8,128)(2,1)S(1)}, u32[]{:S(2)}) copy-start(bf16[128,960]{0,1:T(8,128)(2,1)S(1)} %multiply_convert_fusion.8) | copy-start | bytes 737284
  304.7 59.6 %copy-start.30 = (bf16[128,2560]{1,0:T(8,128)(2,1)}, bf16[128,2560]{1,0:T(8,128)(2,1)S(1)}, u32[]{:S(2)}) copy-start(bf16[128,2560]{1,0:T(8,128)(2,1)S(1)} %get-tuple-element.781) | copy-start | bytes 1966084
  364.2 155.3 %copy-start.6 = (f32[128,960]{0,1:T(8,128)}, f32[128,960]{0,1:T(8,128)S(1)}, u32[]{:S(2)}) copy-start(f32[128,960]{0,1:T(8,128)S(1)} %get-tuple-element.784) | copy-start | bytes 1474564
  365.2 91.7 %copy-start.44 = (bf16[1,128,960]{1,2,0:T(8,128)(2,1)S(1)}, bf16[1,128,960]{1,2,0:T(8,128)(2,1)}, u32[]{:S(2)}) copy-start(bf16[1,128,960]{1,2,0:T(8,128)(2,1)} %param.22) | copy-start | bytes 737284
  365.9 153.6 %all-gather.48.cloned.1.call-start = ((), (), s32[]{:S(2)}) async-start(), calls=%async_computation.10 | async-start | bytes 2457600 | tf_op jit(solution)/shard_map/all_gather | solution.py:236
  366.5 214.2 %all-gather.52.cloned.1.call-start = ((), (), s32[]{:S(2)}) async-start(), calls=%async_computation.12 | async-start | bytes 6144000 | tf_op jit(solution)/shard_map/all_gather | solution.py:238
  367.3 274.4 %all-gather.50.cloned.1.call-start = ((), (), s32[]{:S(2)}) async-start(), calls=%async_computation.11 | async-start | bytes 6144000 | tf_op jit(solution)/shard_map/all_gather | solution.py:237
  367.9 389.6 %reduce-scatter.7.cloned.1.call-start = ((), (), s32[]{:S(2)}) async-start(), calls=%async_computation.14 | async-start | bytes 1474560
  498.8 86.2 %copy-start.60 = (bf16[128,5,3,64]{0,3,2,1:T(8,128)(2,1)}, bf16[128,5,3,64]{0,3,2,1:T(8,128)(2,1)S(1)}, u32[]{:S(2)}) copy-start(bf16[128,5,3,64]{0,3,2,1:T(8,128)(2,1)S(1)} %bitcast_convert_fusion) | copy-start | bytes 737284
  522.0 129.7 %copy-start.4 = (f32[128,960]{0,1:T(8,128)}, f32[128,960]{0,1:T(8,128)S(1)}, u32[]{:S(2)}) copy-start(f32[128,960]{0,1:T(8,128)S(1)} %get-tuple-element.786) | copy-start | bytes 1474564
  522.2 125.0 %copy-start.26 = (bf16[128,960]{0,1:T(8,128)(2,1)}, bf16[128,960]{0,1:T(8,128)(2,1)S(1)}, u32[]{:S(2)}) copy-start(bf16[128,960]{0,1:T(8,128)(2,1)S(1)} %multiply_convert_fusion.6) | copy-start | bytes 737284
  676.6 222.0 %reduce-scatter.9.cloned.1.call-start = ((), (), s32[]{:S(2)}) async-start(), calls=%async_computation.15 | async-start | bytes 1474560
  800.0 817.0 %all-reduce.14.cloned.1.call-start = ((), (), s32[]{:S(2)}) async-start(), calls=%async_computation.17 | async-start | bytes 78659584
  921.0 14.5 slice-start.6
  942.2 1094.5 %all-reduce.12.cloned.1.call-start = ((), (), s32[]{:S(2)}) async-start(), calls=%async_computation.16 | async-start | bytes 39329792 | tf_op jit(solution)/shard_map/psum | solution.py:197
  1617.0 15.9 copy-start.37
  (71 other events, 349.8 us)
Sparse Core Ops, SparseCore 0:
  66.5 26.1 all-gather.31
  95.1 42.6 all-gather.35
  139.6 38.1 all-gather.37
  180.1 58.6 all-gather.39
  241.1 58.6 all-gather.41
  301.5 58.6 all-gather.43
  362.1 34.2 all-gather.45
  398.2 58.6 all-gather.53
  459.1 25.8 all-gather.33
  486.7 32.7 all-gather.47
  522.0 58.6 all-gather.51
  583.0 58.6 all-gather.49
  676.7 33.1 reduce-scatter.6
  800.1 33.2 reduce-scatter.8
  942.3 674.5 all-reduce.13
  1645.1 391.6 all-reduce.11
where the time goes:
time: 2200 us
  waiting for transfers between devices  1500 us (68%)
  local copies, waits for them, and re-layouts  386 us (18%)
  matrix products  143 us (6%)
  blocking collectives  98.6 us (4%)
  other arithmetic  55.3 us (3%)
    unnamed x19, waiting for transfers between devices  678 us
    psum x1, waiting for transfers between devices, reduce_grads(): lax.psum(mine.astype(jnp.bfloat16), 'ctx').astype(jnp.float32)  385 us
    unnamed x208, local copies, waits for them, and re-layouts  139 us
    all_gather x2, waiting for transfers between devices, on_device(): lax.all_gather(w_up[index], 'fsdp', axis=0, tiled=True)  115 us
    all_gather x2, waiting for transfers between devices, on_device(): lax.all_gather(w_gate[index], 'fsdp', axis=0, tiled=True)  115 us
    all_gather x2, waiting for transfers between devices, on_device(): lax.all_gather(w_down[index], 'fsdp', axis=0, tiled=True)  114 us
    slice x4, local copies, waits for them, and re-layouts, reduce_grads(): mine[offset:offset + amount]  71.2 us
    reshape x18, local copies, waits for them, and re-layouts, reduce_grads(): item.reshape(parts, -1)  66.6 us
  transfers between devices with their start and end apart: 16, of which 12 were waited for; matrix products, arithmetic and copies ran while one was open for 12% of the time, Pallas kernels for 0%

commit v1 on v0

v1 whole, which is shorter than its diff:
```python
import functools

import jax
import jax.numpy as jnp
from jax import lax
from jax.experimental import pallas as pl
from jax.experimental.pallas import tpu as pltpu
from jax.sharding import PartitionSpec as P

QUERY_HEADS = 15
KEY_VALUE_HEADS = 5
HEAD_SIZE = 64
GROUP = QUERY_HEADS // KEY_VALUE_HEADS
QW = QUERY_HEADS * HEAD_SIZE
KVW = KEY_VALUE_HEADS * HEAD_SIZE
PAIR = 2 * KVW
BLK = 64
LANES = 128

EPS = 1e-05
ROPE_BASE = 100000.0
SCORE_FLOOR = -1e30
SCALE = HEAD_SIZE ** (-0.5)


def rope_tables(token_positions):
    half = HEAD_SIZE // 2
    freqs = ROPE_BASE ** (-jnp.arange(half, dtype=jnp.float32) * 2.0 / HEAD_SIZE)
    angles = token_positions.astype(jnp.float32)[:, None] * freqs[None, :]
    cosine, sine = jnp.cos(angles), jnp.sin(angles)
    return (
        jnp.concatenate([cosine, cosine], axis=1),
        jnp.concatenate([-sine, sine], axis=1),
    )


def swap_halves(rows):
    half = HEAD_SIZE // 2
    width = rows.shape[1]
    left = jnp.concatenate([rows[:, half:], rows[:, :half]], axis=1)
    right = jnp.concatenate([rows[:, width - half :], rows[:, : width - half]], axis=1)
    first = (lax.broadcasted_iota(jnp.int32, (1, width), 1) % HEAD_SIZE) < half
    return jnp.where(first, left, right)


def rotate(rows, cosine, sine):
    heads = rows.shape[1] // HEAD_SIZE
    return rows * jnp.tile(cosine, (1, heads)) + swap_halves(rows) * jnp.tile(sine, (1, heads))


def rms_factor(hidden):
    return lax.rsqrt(jnp.mean(hidden * hidden, axis=-1, keepdims=True) + EPS)


def norm_back(hidden, gain, grad_out):
    factor = rms_factor(hidden)
    scaled = grad_out * gain
    grad_gain = jnp.sum(grad_out * hidden * factor, axis=0)
    inner = jnp.mean(hidden * scaled, axis=-1, keepdims=True)
    return (factor * scaled - hidden * (factor * factor * factor) * inner, grad_gain)


def dot(left, right):
    return jnp.dot(left, right, preferred_element_type=jnp.float32)


def dot_t(left, right):
    return lax.dot_general(
        left, right, (((1,), (1,)), ((), ())), preferred_element_type=jnp.float32
    )


def t_dot(left, right):
    return lax.dot_general(
        left, right, (((0,), (0,)), ((), ())), preferred_element_type=jnp.float32
    )


def head_of(rows, index):
    return rows[:, index * HEAD_SIZE : (index + 1) * HEAD_SIZE]


def group_rows(ref, group):
    rows = ref[:, group * GROUP * HEAD_SIZE : (group + 1) * GROUP * HEAD_SIZE]
    return jnp.concatenate([head_of(rows, index) for index in range(GROUP)], axis=0)


def softmax_parts(query, key, visible):
    scores = jnp.where(visible, dot_t(query, key) * SCALE, SCORE_FLOOR)
    top = jnp.max(scores, axis=-1, keepdims=True)
    weights = jnp.where(visible, jnp.exp(scores - top), 0.0)
    return weights, jnp.sum(weights, axis=-1, keepdims=True)


def attend_kernel(query_ref, pair_ref, query_place_ref, key_place_ref, mixed_ref):
    tokens = query_ref.shape[0]
    visible = key_place_ref[...] <= query_place_ref[...]
    visible = jnp.concatenate([visible.astype(jnp.float32)] * GROUP, axis=0) > 0.5
    for group in range(KEY_VALUE_HEADS):
        key = pair_ref[:, group * HEAD_SIZE : (group + 1) * HEAD_SIZE]
        value = pair_ref[:, KVW + group * HEAD_SIZE : KVW + (group + 1) * HEAD_SIZE]
        weights, total = softmax_parts(group_rows(query_ref, group), key, visible)
        mixed = dot(weights.astype(jnp.bfloat16), value) / total
        mixed_ref[:, group * GROUP * HEAD_SIZE : (group + 1) * GROUP * HEAD_SIZE] = (
            jnp.concatenate(
                [mixed[index * tokens : (index + 1) * tokens] for index in range(GROUP)], axis=1
            )
        )


def attend_back_kernel(
    query_ref,
    pair_ref,
    query_place_ref,
    key_place_ref,
    mixed_ref,
    mixed_grad_ref,
    query_grad_ref,
    pair_grad_ref,
):
    tokens = query_ref.shape[0]
    visible = key_place_ref[...] <= query_place_ref[...]
    visible = jnp.concatenate([visible.astype(jnp.float32)] * GROUP, axis=0) > 0.5
    for group in range(KEY_VALUE_HEADS):
        key_at = slice(group * HEAD_SIZE, (group + 1) * HEAD_SIZE)
        value_at = slice(KVW + group * HEAD_SIZE, KVW + (group + 1) * HEAD_SIZE)
        key = pair_ref[:, key_at]
        value = pair_ref[:, value_at]
        query = group_rows(query_ref, group)
        mixed_grad = group_rows(mixed_grad_ref, group)
        delta = jnp.sum(
            mixed_grad.astype(jnp.float32) * group_rows(mixed_ref, group), axis=-1, keepdims=True
        )
        weights, total = softmax_parts(query, key, visible)
        probs = weights / total
        pair_grad_ref[:, value_at] = t_dot(probs.astype(jnp.bfloat16), mixed_grad).astype(
            jnp.bfloat16
        )
        grad_scores = (probs * (dot_t(mixed_grad, value) - delta)).astype(jnp.bfloat16)
        pair_grad_ref[:, key_at] = (t_dot(grad_scores, query) * SCALE).astype(jnp.bfloat16)
        query_grad = dot(grad_scores, key) * SCALE
        query_grad_ref[:, group * GROUP * HEAD_SIZE : (group + 1) * GROUP * HEAD_SIZE] = (
            jnp.concatenate(
                [query_grad[index * tokens : (index + 1) * tokens] for index in range(GROUP)],
                axis=1,
            )
        )


def kernel_call(kernel, outs, flops):
    return pl.pallas_call(
        kernel,
        out_shape=outs,
        compiler_params=pltpu.CompilerParams(vmem_limit_bytes=48 * 1024 * 1024),
        cost_estimate=pl.CostEstimate(flops=flops, bytes_accessed=6_000_000, transcendentals=0),
    )


def attend(query, pairs, query_place, key_place):
    tokens, keys = query.shape[0], pairs.shape[0]
    return kernel_call(
        attend_kernel,
        jax.ShapeDtypeStruct((tokens, QW), jnp.float32),
        4 * tokens * keys * QW * 4,
    )(query, pairs, query_place, key_place)


def attend_back(query, pairs, query_place, key_place, mixed, mixed_grad):
    tokens, keys = query.shape[0], pairs.shape[0]
    return kernel_call(
        attend_back_kernel,
        (
            jax.ShapeDtypeStruct((tokens, QW), jnp.float32),
            jax.ShapeDtypeStruct((keys, PAIR), jnp.bfloat16),
        ),
        10 * tokens * keys * QW * 4,
    )(query, pairs, query_place, key_place, mixed, mixed_grad)


def gather(item, axis_name):
    return lax.all_gather(item, axis_name, axis=0, tiled=True)


def scatter_sum(item, axis_name):
    return lax.psum_scatter(item, axis_name, scatter_dimension=0, tiled=True)


def on_device(
    tokens,
    positions,
    cotangent,
    w_query,
    w_key,
    w_value,
    w_out,
    w_gate,
    w_up,
    w_down,
    gain_attn,
    gain_mlp,
):
    layers, rows, width = w_query.shape[0], w_query.shape[1], w_query.shape[2]
    split = lax.axis_size("fsdp")
    ff_part = w_down.shape[1]
    low = jnp.bfloat16
    token_positions = positions[0]
    token_rows = token_positions.shape[0]
    cosine, sine = rope_tables(token_positions)
    query_place = token_positions[:, None]

    attn_parts = [
        gather(
            jnp.concatenate([w_query[l], w_key[l], w_value[l], w_out[l]], axis=1), "fsdp"
        )
        for l in range(layers)
    ]
    gains = lax.all_gather(jnp.concatenate([gain_attn, gain_mlp], axis=0), "fsdp", axis=1, tiled=True)
    attn_gains, mlp_gains = gains[:layers], gains[layers:]

    def columns(l):
        pieces = jnp.stack(
            [
                jnp.concatenate(
                    [
                        w_gate[l][:, part * ff_part : (part + 1) * ff_part],
                        w_up[l][:, part * ff_part : (part + 1) * ff_part],
                    ],
                    axis=1,
                )
                for part in range(split)
            ]
        )
        return lax.all_to_all(pieces, "fsdp", 0, 0, tiled=True).reshape(
            split * rows, 2 * ff_part
        )

    gate_up = [columns(l) for l in range(layers)]

    hidden = tokens[0].astype(jnp.float32)
    saved = []
    key_place = None
    for l in range(layers):
        w_qkv = attn_parts[l][:, : QW + PAIR]
        w_o = attn_parts[l][:, QW + PAIR :]
        normed = (hidden * rms_factor(hidden) * attn_gains[l]).astype(low)
        qkv = dot(normed, w_qkv)
        rotated = rotate(qkv[:, : QW + KVW], cosine, sine)
        query = rotated[:, :QW].astype(low)
        pairs = jnp.concatenate([rotated[:, QW:], qkv[:, QW + KVW :]], axis=1).astype(low)
        if key_place is None:
            places = jnp.stack([token_positions // BLK, token_positions % BLK], axis=1)
            places = jnp.pad(places.astype(low), ((0, 0), (0, LANES - 2)))
            all_pairs = gather(jnp.concatenate([pairs, places], axis=1), "ctx")
            key_place = (
                all_pairs[:, PAIR].astype(jnp.int32) * BLK
                + all_pairs[:, PAIR + 1].astype(jnp.int32)
            )[None, :]
            all_pairs = all_pairs[:, :PAIR]
        else:
            all_pairs = gather(pairs, "ctx")
        mixed = attend(query, all_pairs, query_place, key_place)
        mixed_low = mixed.astype(low)
        middle = hidden + dot(mixed_low, w_o)
        normed_mlp = gather((middle * rms_factor(middle) * mlp_gains[l]).astype(low), "fsdp")
        gate_and_up = dot(normed_mlp, gate_up[l])
        gate, up = gate_and_up[:, :ff_part], gate_and_up[:, ff_part:]
        inner = (jax.nn.silu(gate) * up).astype(low)
        saved.append(
            (hidden, normed, query, all_pairs, mixed, mixed_low, middle, normed_mlp, gate, up, inner)
        )
        hidden = middle + scatter_sum(dot(inner, w_down[l]).astype(low), "fsdp").astype(jnp.float32)
    output = hidden.astype(low)[None]

    grad = cotangent[0].astype(jnp.float32)
    collected = [None] * layers
    for l in reversed(range(layers)):
        (hidden, normed, query, all_pairs, mixed, mixed_low, middle, normed_mlp, gate, up, inner) = (
            saved[l]
        )
        w_qkv = attn_parts[l][:, : QW + PAIR]
        w_o = attn_parts[l][:, QW + PAIR :]
        grad_low = gather(grad.astype(low), "fsdp")
        grad_down = t_dot(inner, grad_low).astype(low)
        grad_inner = dot_t(grad_low, w_down[l])
        sigma = jax.nn.sigmoid(gate)
        d_up = (grad_inner * gate * sigma).astype(low)
        d_gate = (grad_inner * up * sigma * (1.0 + gate * (1.0 - sigma))).astype(low)
        d_both = jnp.concatenate([d_gate, d_up], axis=1)
        grad_normed_mlp = scatter_sum(dot_t(d_both, gate_up[l]).astype(low), "fsdp")
        grad_gate_up = t_dot(normed_mlp, d_both).astype(low)
        grad_middle, grad_mlp_gain = norm_back(
            middle, mlp_gains[l].astype(jnp.float32), grad_normed_mlp.astype(jnp.float32)
        )
        grad_middle = grad_middle + grad
        branch_low = grad_middle.astype(low)
        grad_out = t_dot(mixed_low, branch_low).astype(low)
        mixed_grad = dot_t(branch_low, w_o).astype(low)
        query_grad, pair_terms = attend_back(
            query, all_pairs, query_place, key_place, mixed, mixed_grad
        )
        pair_grad = scatter_sum(pair_terms, "ctx").astype(jnp.float32)
        qk_grad = rotate(
            jnp.concatenate([query_grad, pair_grad[:, :KVW]], axis=1), cosine, -sine
        )
        qkv_grad = jnp.concatenate([qk_grad, pair_grad[:, KVW:]], axis=1).astype(low)
        grad_qkv = t_dot(normed, qkv_grad).astype(low)
        grad_normed = dot_t(qkv_grad, w_qkv)
        grad_hidden, grad_attn_gain = norm_back(
            hidden, attn_gains[l].astype(jnp.float32), grad_normed
        )
        grad = grad_hidden + grad_middle
        exchanged = lax.all_to_all(
            grad_gate_up.reshape(split, rows, 2 * ff_part), "fsdp", 0, 0, tiled=True
        )
        exchanged = exchanged.reshape(split * rows, 2 * ff_part)
        attn_grads = scatter_sum(jnp.concatenate([grad_qkv, grad_out], axis=1), "fsdp")
        mlp_sum = lax.psum(exchanged, "ctx").reshape(split, rows, 2 * ff_part)
        down_sum = lax.psum(grad_down, "ctx")
        attn_sum = lax.psum(attn_grads, "ctx")
        collected[l] = (
            attn_sum[:, :QW],
            attn_sum[:, QW : QW + KVW],
            attn_sum[:, QW + KVW : QW + PAIR],
            attn_sum[:, QW + PAIR :],
            jnp.concatenate([mlp_sum[part, :, :ff_part] for part in range(split)], axis=1),
            jnp.concatenate([mlp_sum[part, :, ff_part:] for part in range(split)], axis=1),
            down_sum,
            grad_attn_gain,
            grad_mlp_gain,
        )
    grad_tokens = grad.astype(low)[None]
    gain_sums = scatter_sum(
        jnp.stack([collected[l][at] for at in (7, 8) for l in range(layers)], axis=1), "fsdp"
    )
    gain_sums = lax.psum(gain_sums, "ctx").T
    stacked = [
        jnp.stack([collected[l][member].astype(jnp.float32) for l in range(layers)])
        for member in range(7)
    ]
    return (output, grad_tokens, *stacked, gain_sums[:layers], gain_sums[layers:])


def solution(mesh):
    rows = P("fsdp", "ctx", None)
    weight = P(None, "fsdp", None)
    gain = P(None, "fsdp")
    return jax.shard_map(
        on_device,
        mesh=mesh,
        in_specs=(rows, P("fsdp", "ctx"), rows) + (weight,) * 7 + (gain,) * 2,
        out_specs=(rows, rows) + (weight,) * 7 + (gain,) * 2,
        check_vma=False,
    )
```

time: 2200 us -> 980 us (0.45)
  waiting for transfers between devices: 1500 us -> 578 us
  local copies, waits for them, and re-layouts: 386 us -> 95.8 us
  matrix products: 143 us -> 68.3 us
  Pallas kernels: 0 us -> 28.2 us
    unnamed x19 -> x17, waiting for transfers between devices: 678 us -> 95.9 us
    all_gather x12 -> x4, waiting for transfers between devices: 433 us -> 116 us  [gather(): return lax.all_gather(item, axis_name, axis=0, tiled=True)]
    psum x1, waiting for transfers between devices: 385 us -> 172 us  [on_device(): attn_sum = lax.psum(attn_grads, 'ctx')]
    reduce_scatter x0 -> x4, waiting for transfers between devices: none -> 117 us  [scatter_sum(): return lax.psum_scatter(item, axis_name, scatter_dimension=0, tiled=True)]
    unnamed x208 -> x240, local copies, waits for them, and re-layouts: 139 us -> 55.5 us
    all_to_all x0 -> x4, waiting for transfers between devices: none -> 77 us  [the longest x2 77 us: on_device(): lax.all_to_all(grad_gate_up.reshape(split, rows, 2 * ff_part), 'fsdp', 0,...]
    dot_general x70 -> x24, matrix products: 143 us -> 68.3 us  [the longest x8 26.8 us: dot(): return jnp.dot(left, right, preferred_element_type=jnp.float32)]
    reshape x21 -> x0, local copies, waits for them, and re-layouts: 70.5 us -> none  [the longest x18 66.6 us: reduce_grads(): item.reshape(parts, -1)]
  transfers between devices with their start and end apart: 16 -> 17, of which waited for: 12 -> 14; matrix products, arithmetic and copies ran while one was open for 12% -> 9% of each run, Pallas kernels for 0% -> 1%
where the time goes in v1:
time: 980 us; the launch traced here: 972 us
  waiting for transfers between devices  578 us (59%)
  blocking collectives  118 us (12%)
  local copies, waits for them, and re-layouts  95.8 us (10%)
  matrix products  68.3 us (7%)
  other arithmetic  47.8 us (5%)
  Pallas kernels  28.2 us (3%)
  starting transfers between devices  19.6 us (2%)
  between operations  16.2 us (2%)
    psum x1, waiting for transfers between devices, on_device(): attn_sum = lax.psum(attn_grads, 'ctx')  172 us
    reduce_scatter x4, waiting for transfers between devices, scatter_sum(): return lax.psum_scatter(item, axis_name, scatter_dimension=0, tiled=True)  117 us
    all_gather x4, waiting for transfers between devices, gather(): return lax.all_gather(item, axis_name, axis=0, tiled=True)  116 us
    unnamed x17, waiting for transfers between devices  95.9 us
    all_gather x4, blocking collectives, gather(): return lax.all_gather(item, axis_name, axis=0, tiled=True)  78.8 us
    all_to_all x2, waiting for transfers between devices, on_device(): lax.all_to_all(grad_gate_up.reshape(split, rows, 2 * ff_part), 'fsdp', 0,...  77 us
    unnamed x240, local copies, waits for them, and re-layouts  55.5 us
    dot_general x8, matrix products, dot(): return jnp.dot(left, right, preferred_element_type=jnp.float32)  26.8 us
  transfers between devices with their start and end apart: 17, of which 14 were waited for; matrix products, arithmetic and copies ran while one was open for 9% of the time, Pallas kernels for 1%

profile of v1, /device:TPU:0, one launch (start us, length us, event | category | flops | bytes accessed | tf_op | source)
XLA Modules:
  0.0 971.8 jit_solution(14880292010844365287)
XLA Ops:
  14.4 9.7 all-gather.1
  30.2 45.6 %all-gather.7.cloned.1.call-done = bf16[960,2560]{1,0:T(8,128)(2,1)} async-done(((bf16[240,2560]{1,0:T(8,128)(2,1)}), bf16[960,2560]{1,0:T(8,128)(2,1)}) %all-gather.7.cloned.1.call-update) | async-done | bytes 4915216 | tf_op jit(solution)/shard_map/all_gather | solution.py:181
  91.8 4.7 all-to-all-start
  96.9 13.5 %all-gather.9.cloned.1.call-done = bf16[1024,768]{1,0:T(8,128)(2,1)} async-done(((bf16[128,768]{1,0:T(8,128)(2,1)}), bf16[1024,768]{1,0:T(8,128)(2,1)}) %all-gather.9.cloned.1.call-update) | async-done | bytes 1572880 | tf_op jit(solution)/shard_map/all_gather | solution.py:181
  113.1 4.3 shard_map.203.mixed_ref
  121.7 15.2 %all_gather.30 = bf16[512,960]{0,1:T(8,128)(2,1)} all-gather(bf16[128,960]{0,1:T(8,128)(2,1)S(1)} %multiply_convert_fusion.8), channel_id=1, replica_groups=mesh['fsdp'=4,'ctx'=8] {'fsdp'}, dimensions={0}, use_global_device_ids=true | all-gather | bytes 1228800 | tf_op jit(solution)/shard_map/all_gather | solution.py:181
  155.0 20.1 %reduce-scatter.26.cloned.1.call-done = bf16[128,960]{1,0:T(8,128)(2,1)} async-done(((bf16[512,960]{1,0:T(8,128)(2,1)}), bf16[128,960]{1,0:T(8,128)(2,1)}) %reduce-scatter.26.cloned.1.call-update) | async-done | bytes 245776
  179.2 57.0 %all-gather.11.cloned.1.call-done = bf16[960,2560]{1,0:T(8,128)(2,1)} async-done(((bf16[240,2560]{1,0:T(8,128)(2,1)}), bf16[960,2560]{1,0:T(8,128)(2,1)}) %all-gather.11.cloned.1.call-update) | async-done | bytes 4915216 | tf_op jit(solution)/shard_map/all_gather | solution.py:181
  262.1 4.7 all-to-all-start.1
  266.8 38.6 %all-gather = bf16[1,512,960]{1,2,0:T(8,128)(2,1)} all-gather(bf16[1,128,960]{1,2,0:T(8,128)(2,1)S(1)} %copy-done.63), channel_id=2, replica_groups=mesh['fsdp'=4,'ctx'=8] {'fsdp'}, dimensions={1}, use_global_device_ids=true | all-gather | bytes 1228800 | tf_op jit(solution)/shard_map/all_gather | solution.py:181
  306.8 4.3 shard_map.204.mixed_ref
  314.8 12.0 %all_gather.33 = bf16[512,960]{0,1:T(8,128)(2,1)} all-gather(bf16[128,960]{0,1:T(8,128)(2,1)S(1)} %multiply_convert_fusion.6), channel_id=1, replica_groups=mesh['fsdp'=4,'ctx'=8] {'fsdp'}, dimensions={0}, use_global_device_ids=true | all-gather | bytes 1228800 | tf_op jit(solution)/shard_map/all_gather | solution.py:181
  334.0 4.1 convolution_convert_fusion.9
  346.3 22.2 %reduce-scatter.30.cloned.1.call-done = bf16[128,960]{1,0:T(8,128)(2,1)} async-done(((bf16[512,960]{1,0:T(8,128)(2,1)}), bf16[128,960]{1,0:T(8,128)(2,1)}) %reduce-scatter.30.cloned.1.call-update) | async-done | bytes 245776
  372.2 27.5 %reduce-scatter.28.cloned.1.call-done = bf16[128,960]{1,0:T(8,128)(2,1)} async-done(((bf16[512,960]{1,0:T(8,128)(2,1)}), bf16[128,960]{1,0:T(8,128)(2,1)}) %reduce-scatter.28.cloned.1.call-update) | async-done | bytes 245776
  409.9 9.8 %shard_map.205 = (f32[128,960]{1,0:T(8,128)S(1)}, bf16[1024,640]{1,0:T(8,128)(2,1)S(1)}) custom-call(bf16[128,960]{1,0:T(8,128)(2,1)S(1)} %slice.474.query_ref, bf16[1024,640]{1,0:T(8,128)(2,1)S(1)} %copy-done.4, s32[128,1]{1,0:T(8,128)S(1)} %copy.134.query_place_ref, s32[1,1024]{1,0:T(1,128)S(1)} %bitcast.151, f32[128,960]{1,0:T(8,128)S(1)} %shard_map.204.mixed_ref, ...), custom_call_target="tpu_custom_call" | custom-call | flops 5033164800 | bytes 6000000 | tf_op jit(solution)/shard_map/pallas_call | solution.py:170
  424.3 29.9 %reduce-scatter.18.cloned.1.call-done = bf16[128,640]{1,0:T(8,128)(2,1)} async-done(((bf16[1024,640]{1,0:T(8,128)(2,1)}), bf16[128,640]{1,0:T(8,128)(2,1)}) %reduce-scatter.18.cloned.1.call-update) | async-done | bytes 163856 | tf_op jit(solution)/shard_map/reduce_scatter | solution.py:185
  461.5 13.1 %all_gather.35 = bf16[512,960]{0,1:T(8,128)(2,1)S(1)} all-gather(bf16[128,960]{0,1:T(8,128)(2,1)S(1)} %get-tuple-element.77), channel_id=1, replica_groups=mesh['fsdp'=4,'ctx'=8] {'fsdp'}, dimensions={0}, use_global_device_ids=true | all-gather | bytes 1228800 | tf_op jit(solution)/shard_map/all_gather | solution.py:181
  477.0 4.1 convolution_convert_fusion.8
  483.5 25.9 %reduce-scatter.32.cloned.1.call-done = bf16[128,960]{1,0:T(8,128)(2,1)} async-done(((bf16[512,960]{1,0:T(8,128)(2,1)}), bf16[128,960]{1,0:T(8,128)(2,1)}) %reduce-scatter.32.cloned.1.call-update) | async-done | bytes 245776
  516.2 9.8 %shard_map.206 = (f32[128,960]{1,0:T(8,128)S(1)}, bf16[1024,640]{1,0:T(8,128)(2,1)S(1)}) custom-call(bf16[128,960]{1,0:T(8,128)(2,1)S(1)} %slice.449.query_ref, bf16[1024,640]{1,0:T(8,128)(2,1)S(1)} %slice.452.pair_ref, s32[128,1]{1,0:T(8,128)S(1)} %copy.134.query_place_ref, s32[1,1024]{1,0:T(1,128)S(1)} %bitcast.152, f32[128,960]{1,0:T(8,128)S(1)} %shard_map.203.mixed_ref, ...), custom_call_target="tpu_custom_call" | custom-call | flops 5033164800 | bytes 6000000 | tf_op jit(solution)/shard_map/pallas_call | solution.py:170
  536.8 23.7 %reduce-scatter.20.cloned.1.call-done = bf16[128,640]{1,0:T(8,128)(2,1)} async-done(((bf16[1024,640]{1,0:T(8,128)(2,1)}), bf16[128,640]{1,0:T(8,128)(2,1)}) %reduce-scatter.20.cloned.1.call-update) | async-done | bytes 163856 | tf_op jit(solution)/shard_map/reduce_scatter | solution.py:185
  565.8 3.8 pad_maximum_fusion
  577.9 4.2 convolution_convert_fusion.1
  582.1 41.2 %all-to-all-done.3 = bf16[4,240,1280]{2,1,0:T(8,128)(2,1)S(1)} async-done(((bf16[4,240,1280]{2,1,0:T(8,128)(2,1)}), bf16[4,240,1280]{2,1,0:T(8,128)(2,1)S(1)}, u32[]{:S(2)}, u32[]{:S(2)}) %all-to-all-start.3) | async-done | bytes 2457632 | tf_op jit(solution)/shard_map/all_to_all | solution.py:312
  624.7 4.5 all-to-all-start.2
  634.5 35.7 %all-to-all-done.2 = bf16[4,240,1280]{2,1,0:T(8,128)(2,1)} async-done(((bf16[4,240,1280]{2,1,0:T(8,128)(2,1)}), bf16[4,240,1280]{2,1,0:T(8,128)(2,1)}, u32[]{:S(2)}, u32[]{:S(2)}) %all-to-all-start.2) | async-done | bytes 2457632 | tf_op jit(solution)/shard_map/all_to_all | solution.py:312
  671.5 62.0 %reduce-scatter.22.cloned.1.call-done = bf16[240,2560]{1,0:T(8,128)(2,1)} async-done(((bf16[960,2560]{1,0:T(8,128)(2,1)}), bf16[240,2560]{1,0:T(8,128)(2,1)}) %reduce-scatter.22.cloned.1.call-update) | async-done | bytes 1228816 | tf_op jit(solution)/shard_map/reduce_scatter | solution.py:185
  738.6 15.1 %all-reduce.1 = f32[960,4]{0,1:T(4,128)S(1)} all-reduce(f32[960,4]{0,1:T(4,128)S(1)} %pad_maximum_fusion.21), channel_id=11, replica_groups=mesh['fsdp'=4,'ctx'=8] {'fsdp'}, use_global_device_ids=true, to_apply=%region_26.27.clone | all-reduce | flops 3840 | bytes 30720
  753.7 14.8 %psum.55 = f32[4,240]{1,0:T(4,128)S(1)} all-reduce(f32[4,240]{1,0:T(4,128)S(1)} %dynamic-slice_bitcast_fusion), channel_id=1, replica_groups=mesh['fsdp'=4,'ctx'=8] {'ctx'}, use_global_device_ids=true, to_apply=%region_27.28 | all-reduce | flops 960 | bytes 7680 | tf_op jit(solution)/shard_map/psum | solution.py:335
  770.0 171.8 %all-reduce.5.cloned.1.call-done = (bf16[240,2560]{1,0:T(8,128)(2,1)}, bf16[240,2560]{1,0:T(8,128)(2,1)}, bf16[4,240,1280]{2,1,0:T(8,128)(2,1)}, bf16[4,240,1280...) async-done(((bf16[240,2560]{1,0:T(8,128)(2,1)}, bf16[240,2560]{1,0:T(8,128)(2,1)}, bf16[4,240,1280]{2,1,0:T(8,128)(2,1)}, ...) | async-done | bytes 9830416 | tf_op jit(solution)/shard_map/psum | solution.py:319
  952.7 4.2 maximum_convert_fusion.2
  (396 shorter events, 198.7 us)
Async XLA Ops:
  7.2 68.7 %all-gather.7.cloned.1.call-start = ((), (), s32[]{:S(2)}) async-start(), calls=%async_computation.12 | async-start | bytes 6144000 | tf_op jit(solution)/shard_map/all_gather | solution.py:181
  14.3 96.1 %all-gather.9.cloned.1.call-start = ((), (), s32[]{:S(2)}) async-start(), calls=%async_computation.13 | async-start | bytes 1769472 | tf_op jit(solution)/shard_map/all_gather | solution.py:181
  25.2 226.6 %copy-start.5 = (f32[128,1280]{1,0:T(8,128)}, f32[128,1280]{1,0:T(8,128)S(1)}, u32[]{:S(2)}) copy-start(f32[128,1280]{1,0:T(8,128)S(1)} %copy.126) | copy-start | bytes 1966084
  25.6 57.5 %copy-start.17 = (f32[128,1280]{1,0:T(8,128)}, f32[128,1280]{1,0:T(8,128)S(1)}, u32[]{:S(2)}) copy-start(f32[128,1280]{1,0:T(8,128)S(1)} %copy.131) | copy-start | bytes 1966084
  26.4 49.5 %copy-start.86 = (f32[128]{0:T(128)}, f32[128]{0:T(128)S(1)}, u32[]{:S(2)}) copy-start(f32[128]{0:T(128)S(1)} %get-tuple-element.164) | copy-start | bytes 1540
  27.0 48.9 %copy-start.77 = (f32[1,960]{1,0:T(1,128)}, f32[1,960]{1,0:T(1,128)S(1)}, u32[]{:S(2)}) copy-start(f32[1,960]{1,0:T(1,128)S(1)} %get-tuple-element.157) | copy-start | bytes 11524
  91.8 45.1 %all-to-all-start = ((bf16[4,240,1280]{2,1,0:T(8,128)(2,1)}), bf16[4,240,1280]{2,1,0:T(8,128)(2,1)}, u32[]{:S(2)}, u32[]{:S(2)}) async-start(bf16[4,240,1280]{2,1,0:T(8,128)(2,1)} %pad_maximum_fusion.2), calls=%async_computation | async-start | bytes 4915200 | tf_op jit(solution)/shard_map/all_to_all | solution.py:233
  96.5 78.6 %reduce-scatter.26.cloned.1.call-start = ((), (), s32[]{:S(2)}) async-start(), calls=%async_computation.20 | async-start | bytes 1310720
  121.0 55.9 %copy-start.8 = (f32[128,960]{0,1:T(8,128)}, f32[128,960]{0,1:T(8,128)S(1)}, u32[]{:S(2)}) copy-start(f32[128,960]{0,1:T(8,128)S(1)} %get-tuple-element.174) | copy-start | bytes 1474564
  148.1 88.1 %all-gather.11.cloned.1.call-start = ((), (), s32[]{:S(2)}) async-start(), calls=%async_computation.14 | async-start | bytes 6144000 | tf_op jit(solution)/shard_map/all_gather | solution.py:181
  150.9 85.3 %copy-start.79 = (f32[1,960]{1,0:T(1,128)S(1)}, f32[1,960]{1,0:T(1,128)}, u32[]{:S(2)}) copy-start(f32[1,960]{1,0:T(1,128)} %get-tuple-element.155) | copy-start | bytes 11524
  154.5 151.0 %all-gather.13.cloned.1.call-start = ((), (), s32[]{:S(2)}) async-start(), calls=%async_computation.15 | async-start | bytes 1474560 | tf_op jit(solution)/shard_map/all_gather | solution.py:181
  179.2 61.8 %copy-start.88 = (f32[128]{0:T(128)}, f32[128]{0:T(128)S(1)}, u32[]{:S(2)}) copy-start(f32[128]{0:T(128)S(1)} %get-tuple-element.168) | copy-start | bytes 1540
  262.1 43.3 %copy-start.40 = (bf16[128,1280]{1,0:T(8,128)(2,1)S(1)}, bf16[128,1280]{1,0:T(8,128)(2,1)}, u32[]{:S(2)}) copy-start(bf16[128,1280]{1,0:T(8,128)(2,1)} %copy-done.39) | copy-start | bytes 983044
  262.1 64.8 %all-to-all-start.1 = ((bf16[4,240,1280]{2,1,0:T(8,128)(2,1)}), bf16[4,240,1280]{2,1,0:T(8,128)(2,1)}, u32[]{:S(2)}, u32[]{:S(2)}) async-start(bf16[4,240,1280]{2,1,0:T(8,128)(2,1)} %pad_maximum_fusion.3), calls=%async_computation.1 | async-start | bytes 4915200 | tf_op jit(solution)/shard_map/all_to_all | solution.py:233
  266.8 101.7 %reduce-scatter.30.cloned.1.call-start = ((), (), s32[]{:S(2)}) async-start(), calls=%async_computation.22 | async-start | bytes 1310720
  340.3 59.4 %reduce-scatter.28.cloned.1.call-start = ((), (), s32[]{:S(2)}) async-start(), calls=%async_computation.21 | async-start | bytes 1310720
  346.1 108.2 %reduce-scatter.18.cloned.1.call-start = ((), (), s32[]{:S(2)}) async-start(), calls=%async_computation.16 | async-start | bytes 1474560 | tf_op jit(solution)/shard_map/reduce_scatter | solution.py:185
  420.8 88.6 %reduce-scatter.32.cloned.1.call-start = ((), (), s32[]{:S(2)}) async-start(), calls=%async_computation.23 | async-start | bytes 1310720
  481.1 29.4 %copy-start.9 = (f32[128,960]{0,1:T(8,128)S(1)}, f32[128,960]{0,1:T(8,128)}, u32[]{:S(2)}) copy-start(f32[128,960]{0,1:T(8,128)} %copy-done.8) | copy-start | bytes 1474564
  481.1 29.4 %copy-start.84 = (f32[128]{0:T(128)S(1)}, f32[128]{0:T(128)}, u32[]{:S(2)}) copy-start(f32[128]{0:T(128)} %copy-done.83) | copy-start | bytes 1540
  481.1 30.4 %copy-start.94 = (f32[128]{0:T(128)S(1)}, f32[128]{0:T(128)}, u32[]{:S(2)}) copy-start(f32[128]{0:T(128)} %get-tuple-element.165) | copy-start | bytes 1540
  483.5 77.0 %reduce-scatter.20.cloned.1.call-start = ((), (), s32[]{:S(2)}) async-start(), calls=%async_computation.17 | async-start | bytes 1474560 | tf_op jit(solution)/shard_map/reduce_scatter | solution.py:185
  527.1 144.4 %reduce-scatter.24.cloned.1.call-start = ((), (), s32[]{:S(2)}) async-start(), calls=%async_computation.19 | async-start | bytes 6144000 | tf_op jit(solution)/shard_map/reduce_scatter | solution.py:185
  533.8 199.7 %reduce-scatter.22.cloned.1.call-start = ((), (), s32[]{:S(2)}) async-start(), calls=%async_computation.18 | async-start | bytes 6144000 | tf_op jit(solution)/shard_map/reduce_scatter | solution.py:185
  534.8 28.8 %copy-start.7 = (f32[128,1280]{1,0:T(8,128)S(1)}, f32[128,1280]{1,0:T(8,128)}, u32[]{:S(2)}) copy-start(f32[128,1280]{1,0:T(8,128)} %copy-done.5) | copy-start | bytes 1966084
  534.8 28.8 %copy-start.20 = (f32[128,1280]{1,0:T(8,128)S(1)}, f32[128,1280]{1,0:T(8,128)}, u32[]{:S(2)}) copy-start(f32[128,1280]{1,0:T(8,128)} %copy.149) | copy-start | bytes 1966084
  574.1 49.2 %all-to-all-start.3 = ((bf16[4,240,1280]{2,1,0:T(8,128)(2,1)}), bf16[4,240,1280]{2,1,0:T(8,128)(2,1)S(1)}, u32[]{:S(2)}, u32[]{:S(2)}) async-start(bf16[4,240,1280]{2,1,0:T(8,128)(2,1)} %bitcast.157), calls=%async_computation.7 | async-start | bytes 4915200 | tf_op jit(solution)/shard_map/all_to_all | solution.py:312
  624.7 45.5 %all-to-all-start.2 = ((bf16[4,240,1280]{2,1,0:T(8,128)(2,1)}), bf16[4,240,1280]{2,1,0:T(8,128)(2,1)}, u32[]{:S(2)}, u32[]{:S(2)}) async-start(bf16[4,240,1280]{2,1,0:T(8,128)(2,1)} %bitcast.156), calls=%async_computation.6 | async-start | bytes 4915200 | tf_op jit(solution)/shard_map/all_to_all | solution.py:312
  629.3 312.5 %all-reduce.5.cloned.1.call-start = ((), (), s32[]{:S(2)}) async-start(), calls=%async_computation.24 | async-start | bytes 19660800 | tf_op jit(solution)/shard_map/psum | solution.py:319
  735.4 33.7 %copy-start.25 = (f32[128,960]{0,1:T(8,128)S(1)}, f32[128,960]{0,1:T(8,128)}, u32[]{:S(2)}) copy-start(f32[128,960]{0,1:T(8,128)} %copy-done.23) | copy-start | bytes 1474564
  735.4 33.7 %copy-start.93 = (f32[128]{0:T(128)S(1)}, f32[128]{0:T(128)}, u32[]{:S(2)}) copy-start(f32[128]{0:T(128)} %get-tuple-element.163) | copy-start | bytes 1540
  (91 other events, 305.4 us)
Sparse Core Ops, SparseCore 0:
  14.4 61.4 all-gather.6
  85.3 25.0 all-gather.8
  148.2 26.8 reduce-scatter.25
  177.5 58.6 all-gather.10
  258.1 23.4 all-gather.12
  340.5 27.9 reduce-scatter.29
  371.9 27.7 reduce-scatter.27
  420.9 33.2 reduce-scatter.17
  483.6 25.7 reduce-scatter.31
  527.2 33.2 reduce-scatter.19
  564.1 107.3 reduce-scatter.23
  675.0 58.4 reduce-scatter.21
  736.9 204.8 all-reduce.4

commit v2 on v1

--- a/solution.py
+++ b/solution.py
@@ -183,6 +183,17 @@
 
 def scatter_sum(item, axis_name):
     return lax.psum_scatter(item, axis_name, scatter_dimension=0, tiled=True)
+
+
+def exchange_sum(item, axis_name):
+    parts = lax.axis_size(axis_name)
+    blocks = item.reshape(parts, item.shape[0] // parts, item.shape[1])
+    blocks = lax.all_to_all(blocks, axis_name, 0, 0, tiled=True)
+    return jnp.sum(blocks.astype(jnp.float32), axis=0)
+
+
+def together(*items):
+    return lax.optimization_barrier(items)
 
 
 def on_device(
@@ -262,17 +273,22 @@
         mixed_low = mixed.astype(low)
         middle = hidden + dot(mixed_low, w_o)
         normed_mlp = gather((middle * rms_factor(middle) * mlp_gains[l]).astype(low), "fsdp")
+        if l + 1 < layers:
+            normed_mlp, attn_parts[l + 1] = together(normed_mlp, attn_parts[l + 1])
         gate_and_up = dot(normed_mlp, gate_up[l])
         gate, up = gate_and_up[:, :ff_part], gate_and_up[:, ff_part:]
         inner = (jax.nn.silu(gate) * up).astype(low)
         saved.append(
             (hidden, normed, query, all_pairs, mixed, mixed_low, middle, normed_mlp, gate, up, inner)
         )
-        hidden = middle + scatter_sum(dot(inner, w_down[l]).astype(low), "fsdp").astype(jnp.float32)
+        partial = dot(inner, w_down[l]).astype(low)
+        if l + 1 < layers:
+            partial, gate_up[l + 1] = together(partial, gate_up[l + 1])
+        hidden = middle + exchange_sum(partial, "fsdp")
     output = hidden.astype(low)[None]
 
     grad = cotangent[0].astype(jnp.float32)
-    collected = [None] * layers
+    waiting, mlp_sums, attn_sums, gain_grads = None, [], [], []
     for l in reversed(range(layers)):
         (hidden, normed, query, all_pairs, mixed, mixed_low, middle, normed_mlp, gate, up, inner) = (
             saved[l]
@@ -286,19 +302,33 @@
         d_up = (grad_inner * gate * sigma).astype(low)
         d_gate = (grad_inner * up * sigma * (1.0 + gate * (1.0 - sigma))).astype(low)
         d_both = jnp.concatenate([d_gate, d_up], axis=1)
-        grad_normed_mlp = scatter_sum(dot_t(d_both, gate_up[l]).astype(low), "fsdp")
+        grad_normed_mlp = exchange_sum(dot_t(d_both, gate_up[l]).astype(low), "fsdp")
         grad_gate_up = t_dot(normed_mlp, d_both).astype(low)
+        exchanged = lax.all_to_all(
+            grad_gate_up.reshape(split, rows, 2 * ff_part), "fsdp", 0, 0, tiled=True
+        )
+        exchanged = exchanged.reshape(split * rows, 2 * ff_part)
         grad_middle, grad_mlp_gain = norm_back(
-            middle, mlp_gains[l].astype(jnp.float32), grad_normed_mlp.astype(jnp.float32)
+            middle, mlp_gains[l].astype(jnp.float32), grad_normed_mlp
         )
         grad_middle = grad_middle + grad
         branch_low = grad_middle.astype(low)
         grad_out = t_dot(mixed_low, branch_low).astype(low)
         mixed_grad = dot_t(branch_low, w_o).astype(low)
+        mixed_grad, exchanged, grad_down = together(mixed_grad, exchanged, grad_down)
+        if waiting is None:
+            mlp_sum, down_sum = lax.psum((exchanged, grad_down), "ctx")
+        else:
+            exchanged, grad_down, attn_grads, mlp_sums[-1] = together(
+                exchanged, grad_down, waiting, mlp_sums[-1]
+            )
+            mlp_sum, down_sum, attn_sum = lax.psum((exchanged, grad_down, attn_grads), "ctx")
+            attn_sums.append(attn_sum)
+        mlp_sums.append((mlp_sum, down_sum))
         query_grad, pair_terms = attend_back(
             query, all_pairs, query_place, key_place, mixed, mixed_grad
         )
-        pair_grad = scatter_sum(pair_terms, "ctx").astype(jnp.float32)
+        pair_grad = exchange_sum(pair_terms, "ctx")
         qk_grad = rotate(
             jnp.concatenate([query_grad, pair_grad[:, :KVW]], axis=1), cosine, -sine
         )
@@ -309,30 +339,29 @@
             hidden, attn_gains[l].astype(jnp.float32), grad_normed
         )
         grad = grad_hidden + grad_middle
-        exchanged = lax.all_to_all(
-            grad_gate_up.reshape(split, rows, 2 * ff_part), "fsdp", 0, 0, tiled=True
-        )
-        exchanged = exchanged.reshape(split * rows, 2 * ff_part)
-        attn_grads = scatter_sum(jnp.concatenate([grad_qkv, grad_out], axis=1), "fsdp")
-        mlp_sum = lax.psum(exchanged, "ctx").reshape(split, rows, 2 * ff_part)
-        down_sum = lax.psum(grad_down, "ctx")
-        attn_sum = lax.psum(attn_grads, "ctx")
-        collected[l] = (
-            attn_sum[:, :QW],
-            attn_sum[:, QW : QW + KVW],
-            attn_sum[:, QW + KVW : QW + PAIR],
-            attn_sum[:, QW + PAIR :],
-            jnp.concatenate([mlp_sum[part, :, :ff_part] for part in range(split)], axis=1),
-            jnp.concatenate([mlp_sum[part, :, ff_part:] for part in range(split)], axis=1),
-            down_sum,
-            grad_attn_gain,
-            grad_mlp_gain,
-        )
+        waiting = scatter_sum(jnp.concatenate([grad_qkv, grad_out], axis=1), "fsdp")
+        gain_grads = [(grad_attn_gain, grad_mlp_gain)] + gain_grads
     grad_tokens = grad.astype(low)[None]
-    gain_sums = scatter_sum(
-        jnp.stack([collected[l][at] for at in (7, 8) for l in range(layers)], axis=1), "fsdp"
-    )
-    gain_sums = lax.psum(gain_sums, "ctx").T
+    gain_sums = lax.psum(
+        jnp.stack([pair[at] for at in (0, 1) for pair in gain_grads]), ("fsdp", "ctx")
+    )
+    gain_sums = lax.dynamic_slice_in_dim(gain_sums, lax.axis_index("fsdp") * rows, rows, 1)
+    attn_grads, gain_sums, mlp_sums[-1] = together(waiting, gain_sums, mlp_sums[-1])
+    attn_sums.append(lax.psum(attn_grads, "ctx"))
+    collected = []
+    for (mlp_sum, down_sum), attn_sum in zip(reversed(mlp_sums), reversed(attn_sums)):
+        mlp_sum = mlp_sum.reshape(split, rows, 2 * ff_part)
+        collected.append(
+            (
+                attn_sum[:, :QW],
+                attn_sum[:, QW : QW + KVW],
+                attn_sum[:, QW + KVW : QW + PAIR],
+                attn_sum[:, QW + PAIR :],
+                jnp.concatenate([mlp_sum[part, :, :ff_part] for part in range(split)], axis=1),
+                jnp.concatenate([mlp_sum[part, :, ff_part:] for part in range(split)], axis=1),
+                down_sum,
+            )
+        )
     stacked = [
         jnp.stack([collected[l][member].astype(jnp.float32) for l in range(layers)])
         for member in range(7)

time: 980 us -> 822 us (0.84)
  waiting for transfers between devices: 578 us -> 358 us
  blocking collectives: 118 us -> 160 us
  starting transfers between devices: 19.6 us -> 51.2 us
  local copies, waits for them, and re-layouts: 95.8 us -> 73.5 us
    unnamed x17 -> x9, waiting for transfers between devices: 95.9 us -> 0.15 us
    psum x1 -> x3, waiting for transfers between devices: 172 us -> 90.2 us  [the longest x2 90.2 us: on_device(): lax.psum((exchanged, grad_down, attn_grads), 'ctx')]
    all_to_all x0 -> x5, waiting for transfers between devices: none -> 58.8 us  [exchange_sum(): blocks = lax.all_to_all(blocks, axis_name, 0, 0, tiled=True)]
    all_gather x4, waiting for transfers between devices: 116 us -> 62.7 us  [gather(): return lax.all_gather(item, axis_name, axis=0, tiled=True)]
    all_to_all x2, waiting for transfers between devices: 77 us -> 33.6 us  [on_device(): lax.all_to_all(grad_gate_up.reshape(split, rows, 2 * ff_part), 'fsdp', 0,...]
    all_to_all x0 -> x5, starting transfers between devices: none -> 31.7 us  [exchange_sum(): blocks = lax.all_to_all(blocks, axis_name, 0, 0, tiled=True)]
    reduce_scatter x4 -> x2, waiting for transfers between devices: 117 us -> 91.3 us  [scatter_sum(): return lax.psum_scatter(item, axis_name, scatter_dimension=0, tiled=True)]
    psum x1, blocking collectives: 14.8 us -> 40.3 us  [on_device(): lax.psum(jnp.stack([pair[at] for at in (0, 1) for pair in gain_grads]), (...]
  transfers between devices with their start and end apart: 17 -> 18, of which waited for: 14 -> 15; matrix products, arithmetic and copies ran while one was open for 9% -> 14% of each run, Pallas kernels for 1% -> 2%
where the time goes in v2:
time: 822 us; the launch traced here: 809 us
  waiting for transfers between devices  358 us (44%)
  blocking collectives  160 us (19%)
  local copies, waits for them, and re-layouts  73.5 us (9%)
  matrix products  72.2 us (9%)
  starting transfers between devices  51.2 us (6%)
  other arithmetic  49.6 us (6%)
  Pallas kernels  28.4 us (3%)
  between operations  15.3 us (2%)
    all_gather x4, blocking collectives, gather(): return lax.all_gather(item, axis_name, axis=0, tiled=True)  97.1 us
    reduce_scatter x2, waiting for transfers between devices, scatter_sum(): return lax.psum_scatter(item, axis_name, scatter_dimension=0, tiled=True)  91.3 us
    psum x2, waiting for transfers between devices, on_device(): lax.psum((exchanged, grad_down, attn_grads), 'ctx')  90.2 us
    all_gather x4, waiting for transfers between devices, gather(): return lax.all_gather(item, axis_name, axis=0, tiled=True)  62.7 us
    all_to_all x5, waiting for transfers between devices, exchange_sum(): blocks = lax.all_to_all(blocks, axis_name, 0, 0, tiled=True)  58.8 us
    psum x1, blocking collectives, on_device(): lax.psum(jnp.stack([pair[at] for at in (0, 1) for pair in gain_grads]), (...  40.3 us
    unnamed x191, local copies, waits for them, and re-layouts  36.4 us
    all_to_all x2, waiting for transfers between devices, on_device(): lax.all_to_all(grad_gate_up.reshape(split, rows, 2 * ff_part), 'fsdp', 0,...  33.6 us
  transfers between devices with their start and end apart: 18, of which 15 were waited for; matrix products, arithmetic and copies ran while one was open for 14% of the time, Pallas kernels for 2%

profile of v2, /device:TPU:0, one launch (start us, length us, event | category | flops | bytes accessed | tf_op | source)
XLA Modules:
  0.0 808.8 jit_solution(11520657059839683704)
XLA Ops:
  15.5 9.5 %all-gather.1 = bf16[4,240,4]{1,2,0:T(4,128)(2,1)S(1)} all-gather(bf16[1,240,4]{1,2,0:T(4,128)(2,1)S(1)} %maximum_bitcast_fusion.8), channel_id=1, replica_groups=mesh['fsdp'=4,'ctx'=8] {'fsdp'}, dimensions={0}, use_global_device_ids=true | all-gather | bytes 9600 | tf_op jit(solution)/shard_map/all_gather | solution.py:228
  26.8 49.0 %all-gather.7.cloned.1.call-done = bf16[960,2560]{1,0:T(8,128)(2,1)} async-done(((bf16[240,2560]{1,0:T(8,128)(2,1)}), bf16[960,2560]{1,0:T(8,128)(2,1)}) %all-gather.7.cloned.1.call-update) | async-done | bytes 4915216 | tf_op jit(solution)/shard_map/all_gather | solution.py:181
  99.6 4.9 all-to-all-start
  108.5 4.8 all-gather.9.cloned.1.call-done
  120.3 21.6 %all-to-all-done = bf16[4,240,1280]{2,1,0:T(8,128)(2,1)} async-done(((bf16[4,240,1280]{2,1,0:T(8,128)(2,1)}), bf16[4,240,1280]{2,1,0:T(8,128)(2,1)}, u32[]{:S(2)}, u32[]{:S(2)}) %all-to-all-start) | async-done | bytes 2457632 | tf_op jit(solution)/shard_map/all_to_all | solution.py:244
  141.9 4.5 all-to-all-start.1
  150.8 57.7 %all_gather.30 = bf16[512,960]{0,1:T(8,128)(2,1)} all-gather(bf16[128,960]{0,1:T(8,128)(2,1)S(1)} %multiply_convert_fusion.8), channel_id=1, replica_groups=mesh['fsdp'=4,'ctx'=8] {'fsdp'}, dimensions={0}, use_global_device_ids=true | all-gather | bytes 1228800 | tf_op jit(solution)/shard_map/all_gather | solution.py:181
  218.8 13.4 %all_to_all.50 = bf16[4,128,960]{1,2,0:T(8,128)(2,1)S(1)} all-to-all(bf16[4,128,960]{1,2,0:T(8,128)(2,1)S(1)} %copy_bitcast_fusion.3), channel_id=1, replica_groups=mesh['fsdp'=4,'ctx'=8] {'fsdp'}, dimensions={0} | all-to-all | bytes 1966080 | tf_op jit(solution)/shard_map/all_to_all | solution.py:191
  253.7 13.1 %all-gather = bf16[1,512,960]{1,2,0:T(8,128)(2,1)} all-gather(bf16[1,128,960]{1,2,0:T(8,128)(2,1)} %param.14), channel_id=2, replica_groups=mesh['fsdp'=4,'ctx'=8] {'fsdp'}, dimensions={1}, use_global_device_ids=true | all-gather | bytes 1228800 | tf_op jit(solution)/shard_map/all_gather | solution.py:181
  267.7 9.0 %all-gather.13.cloned.1.call-done.pair_ref = bf16[1024,640]{1,0:T(8,128)(2,1)} async-done(((bf16[128,640]{1,0:T(8,128)(2,1)}), bf16[1024,640]{1,0:T(8,128)(2,1)}) %all-gather.13.cloned.1.call-update) | async-done | bytes 1310736 | tf_op jit(solution)/shard_map/all_gather | solution.py:181
  278.0 4.3 shard_map.204.mixed_ref
  286.1 13.8 %all_gather.33 = bf16[512,960]{0,1:T(8,128)(2,1)S(1)} all-gather(bf16[128,960]{0,1:T(8,128)(2,1)S(1)} %multiply_convert_fusion.6), channel_id=1, replica_groups=mesh['fsdp'=4,'ctx'=8] {'fsdp'}, dimensions={0}, use_global_device_ids=true | all-gather | bytes 1228800 | tf_op jit(solution)/shard_map/all_gather | solution.py:181
  319.2 8.7 %all-to-all-done.4 = bf16[4,128,960]{1,2,0:T(8,128)(2,1)} async-done(((bf16[4,128,960]{1,2,0:T(8,128)(2,1)}), bf16[4,128,960]{1,2,0:T(8,128)(2,1)}, u32[]{:S(2)}, u32[]{:S(2)}) %all-to-all-start.4) | async-done | bytes 983072 | tf_op jit(solution)/shard_map/all_to_all | solution.py:191
  332.1 4.5 convolution_convert_fusion.3
  336.6 8.0 all-to-all-done.3
  344.6 4.7 all-to-all-start.5
  361.5 15.9 %all-to-all-done.5 = bf16[4,240,1280]{2,1,0:T(8,128)(2,1)} async-done(((bf16[4,240,1280]{2,1,0:T(8,128)(2,1)}), bf16[4,240,1280]{2,1,0:T(8,128)(2,1)}, u32[]{:S(2)}, u32[]{:S(2)}) %all-to-all-start.5) | async-done | bytes 2457632 | tf_op jit(solution)/shard_map/all_to_all | solution.py:307
  379.6 10.0 %shard_map.205 = (f32[128,960]{1,0:T(8,128)S(1)}, bf16[1024,640]{1,0:T(8,128)(2,1)S(1)}) custom-call(bf16[128,960]{1,0:T(8,128)(2,1)S(1)} %slice.481.query_ref, bf16[1024,640]{1,0:T(8,128)(2,1)S(1)} %copy-done.3, s32[128,1]{1,0:T(8,128)S(1)} %copy.138.query_place_ref, s32[1,1024]{1,0:T(1,128)S(1)} %bitcast.168, f32[128,960]{1,0:T(8,128)S(1)} %shard_map.204.mixed_ref, ...), custom_call_target="tpu_custom_call" | custom-call | flops 5033164800 | bytes 6000000 | tf_op jit(solution)/shard_map/pallas_call | solution.py:170
  390.7 4.4 all-to-all-start.6
  401.3 35.8 %all-to-all-done.6 = bf16[8,128,640]{2,1,0:T(8,128)(2,1)} async-done(((bf16[8,128,640]{2,1,0:T(8,128)(2,1)}), bf16[8,128,640]{2,1,0:T(8,128)(2,1)}, u32[]{:S(2)}, u32[]{:S(2)}) %all-to-all-start.6) | async-done | bytes 1310752 | tf_op jit(solution)/shard_map/all_to_all | solution.py:191
  451.3 12.5 %all_gather.35 = bf16[512,960]{0,1:T(8,128)(2,1)S(1)} all-gather(bf16[128,960]{0,1:T(8,128)(2,1)S(1)} %get-tuple-element.115), channel_id=1, replica_groups=mesh['fsdp'=4,'ctx'=8] {'fsdp'}, dimensions={0}, use_global_device_ids=true | all-gather | bytes 1228800 | tf_op jit(solution)/shard_map/all_gather | solution.py:181
  479.2 5.9 all-to-all-done.7
  485.1 5.1 all-to-all-start.8
  498.2 17.7 %all-to-all-done.8 = bf16[4,240,1280]{2,1,0:T(8,128)(2,1)} async-done(((bf16[4,240,1280]{2,1,0:T(8,128)(2,1)}), bf16[4,240,1280]{2,1,0:T(8,128)(2,1)}, u32[]{:S(2)}, u32[]{:S(2)}) %all-to-all-start.8) | async-done | bytes 2457632 | tf_op jit(solution)/shard_map/all_to_all | solution.py:307
  515.9 9.8 %shard_map.206 = (f32[128,960]{1,0:T(8,128)S(1)}, bf16[1024,640]{1,0:T(8,128)(2,1)S(1)}) custom-call(bf16[128,960]{1,0:T(8,128)(2,1)S(1)} %slice.449.query_ref, bf16[1024,640]{1,0:T(8,128)(2,1)S(1)} %slice.452.pair_ref, s32[128,1]{1,0:T(8,128)S(1)} %copy.138.query_place_ref, s32[1,1024]{1,0:T(1,128)S(1)} %bitcast.169, f32[128,960]{1,0:T(8,128)S(1)} %shard_map.203.mixed_ref, ...), custom_call_target="tpu_custom_call" | custom-call | flops 5033164800 | bytes 6000000 | tf_op jit(solution)/shard_map/pallas_call | solution.py:170
  526.8 14.5 %all-to-all-start.9 = ((bf16[8,128,640]{2,1,0:T(8,128)(2,1)}), bf16[8,128,640]{2,1,0:T(8,128)(2,1)}, u32[]{:S(2)}, u32[]{:S(2)}) async-start(bf16[8,128,640]{2,1,0:T(8,128)(2,1)} %bitcast.164), calls=%async_computation.9 | async-start | bytes 2621440 | tf_op jit(solution)/shard_map/all_to_all | solution.py:191
  541.4 29.1 %reduce-scatter.5.cloned.1.call-done = bf16[240,2560]{1,0:T(8,128)(2,1)} async-done(((bf16[960,2560]{1,0:T(8,128)(2,1)}), bf16[240,2560]{1,0:T(8,128)(2,1)}) %reduce-scatter.5.cloned.1.call-update) | async-done | bytes 1228816 | tf_op jit(solution)/shard_map/reduce_scatter | solution.py:185
  586.1 40.3 %psum.49 = f32[4,960]{1,0:T(4,128)S(1)} all-reduce(f32[4,960]{1,0:T(4,128)S(1)} %pad_maximum_fusion.21), channel_id=1, replica_groups=mesh['fsdp'=4,'ctx'=8] {'fsdp','ctx'}, use_global_device_ids=true, to_apply=%region_19.20 | all-reduce | flops 3840 | bytes 30720 | tf_op jit(solution)/shard_map/psum | solution.py:345
  629.6 32.4 %all-reduce.10.cloned.1.call-done = (bf16[960,1280]{1,0:T(8,128)(2,1)}, bf16[640,960]{0,1:T(8,128)(2,1)}) async-done(((bf16[960,1280]{1,0:T(8,128)(2,1)}, bf16[640,960]{0,1:T(8,128)(2,1)}), (bf16[960,1280]{1,0:T(8,128)(2,1)}, bf16[640,960]{0,1:T(8,128)(2,1)})) %all-reduce.10.cloned.1.call-update) | async-done | bytes 3686416 | tf_op jit(solution)/shard_map/psum | solution.py:325
  662.0 62.1 %reduce-scatter.3.cloned.1.call-done = bf16[240,2560]{1,0:T(8,128)(2,1)} async-done(((bf16[960,2560]{1,0:T(8,128)(2,1)}), bf16[240,2560]{1,0:T(8,128)(2,1)}) %reduce-scatter.3.cloned.1.call-update) | async-done | bytes 1228816 | tf_op jit(solution)/shard_map/reduce_scatter | solution.py:185
  726.0 4.3 maximum_convert_fusion.2
  736.1 57.8 %all-reduce.8.cloned.1.call-done = (bf16[240,2560]{1,0:T(8,128)(2,1)}, bf16[240,2560]{1,0:T(8,128)(2,1)}) async-done(((bf16[240,2560]{1,0:T(8,128)(2,1)}, bf16[240,2560]{1,0:T(8,128)(2,1)}), (bf16[240,2560]{1,0:T(8,128)(2,1)}, bf16[240,2560]{1,0:T(8,128)(2,1)})) %all-reduce.8.cloned.1.call-update) | async-done | bytes 2457616 | tf_op jit(solution)/shard_map/psum | solution.py:325
  (353 shorter events, 204.5 us)
Async XLA Ops:
  7.2 68.6 %all-gather.7.cloned.1.call-start = ((), (), s32[]{:S(2)}) async-start(), calls=%async_computation.12 | async-start | bytes 6144000 | tf_op jit(solution)/shard_map/all_gather | solution.py:181
  14.2 11.3 %copy-start.26 = (bf16[1,128,960]{1,2,0:T(8,128)(2,1)S(1)}, bf16[1,128,960]{1,2,0:T(8,128)(2,1)}, u32[]{:S(2)}) copy-start(bf16[1,128,960]{1,2,0:T(8,128)(2,1)} %param.12) | copy-start | bytes 737284
  14.3 99.0 %all-gather.9.cloned.1.call-start = ((), (), s32[]{:S(2)}) async-start(), calls=%async_computation.13 | async-start | bytes 1769472 | tf_op jit(solution)/shard_map/all_gather | solution.py:181
  15.4 69.8 %copy-start.18 = (f32[128,1280]{1,0:T(8,128)}, f32[128,1280]{1,0:T(8,128)S(1)}, u32[]{:S(2)}) copy-start(f32[128,1280]{1,0:T(8,128)S(1)} %copy.135) | copy-start | bytes 1966084
  25.4 224.8 %copy-start.5 = (f32[128,1280]{1,0:T(8,128)}, f32[128,1280]{1,0:T(8,128)S(1)}, u32[]{:S(2)}) copy-start(f32[128,1280]{1,0:T(8,128)S(1)} %copy.130) | copy-start | bytes 1966084
  26.2 53.0 %copy-start.66 = (f32[128]{0:T(128)}, f32[128]{0:T(128)S(1)}, u32[]{:S(2)}) copy-start(f32[128]{0:T(128)S(1)} %get-tuple-element.202) | copy-start | bytes 1540
  26.8 52.5 %copy-start.58 = (f32[1,960]{1,0:T(1,128)}, f32[1,960]{1,0:T(1,128)S(1)}, u32[]{:S(2)}) copy-start(f32[1,960]{1,0:T(1,128)S(1)} %get-tuple-element.195) | copy-start | bytes 11524
  88.1 120.4 %all-gather.11.cloned.1.call-start = ((), (), s32[]{:S(2)}) async-start(), calls=%async_computation.14 | async-start | bytes 6144000 | tf_op jit(solution)/shard_map/all_gather | solution.py:181
  99.6 42.3 %all-to-all-start = ((bf16[4,240,1280]{2,1,0:T(8,128)(2,1)}), bf16[4,240,1280]{2,1,0:T(8,128)(2,1)}, u32[]{:S(2)}, u32[]{:S(2)}) async-start(bf16[4,240,1280]{2,1,0:T(8,128)(2,1)} %pad_maximum_fusion.2), calls=%async_computation | async-start | bytes 4915200 | tf_op jit(solution)/shard_map/all_to_all | solution.py:244
  141.9 75.5 %all-to-all-start.1 = ((bf16[4,240,1280]{2,1,0:T(8,128)(2,1)}), bf16[4,240,1280]{2,1,0:T(8,128)(2,1)}, u32[]{:S(2)}, u32[]{:S(2)}) async-start(bf16[4,240,1280]{2,1,0:T(8,128)(2,1)} %pad_maximum_fusion.3), calls=%async_computation.1 | async-start | bytes 4915200 | tf_op jit(solution)/shard_map/all_to_all | solution.py:244
  146.4 130.3 %all-gather.13.cloned.1.call-start = ((), (), s32[]{:S(2)}) async-start(), calls=%async_computation.15 | async-start | bytes 1474560 | tf_op jit(solution)/shard_map/all_gather | solution.py:181
  150.0 82.3 %copy-start.8 = (f32[128,960]{0,1:T(8,128)}, f32[128,960]{0,1:T(8,128)S(1)}, u32[]{:S(2)}) copy-start(f32[128,960]{0,1:T(8,128)S(1)} %get-tuple-element.212) | copy-start | bytes 1474564
  150.6 61.5 %copy-start.63 = (f32[128]{0:T(128)}, f32[128]{0:T(128)S(1)}, u32[]{:S(2)}) copy-start(f32[128]{0:T(128)S(1)} %get-tuple-element.204) | copy-start | bytes 1540
  218.8 14.3 %copy-start.60 = (f32[1,960]{1,0:T(1,128)S(1)}, f32[1,960]{1,0:T(1,128)}, u32[]{:S(2)}) copy-start(f32[1,960]{1,0:T(1,128)} %get-tuple-element.193) | copy-start | bytes 11524
  311.4 16.5 %all-to-all-start.4 = ((bf16[4,128,960]{1,2,0:T(8,128)(2,1)}), bf16[4,128,960]{1,2,0:T(8,128)(2,1)}, u32[]{:S(2)}, u32[]{:S(2)}) async-start(bf16[4,128,960]{1,2,0:T(8,128)(2,1)} %bitcast.171), calls=%async_computation.4 | async-start | bytes 1966080 | tf_op jit(solution)/shard_map/all_to_all | solution.py:191
  327.9 16.7 %all-to-all-start.3 = ((bf16[4,128,960]{1,2,0:T(8,128)(2,1)}), bf16[4,128,960]{1,2,0:T(8,128)(2,1)}, u32[]{:S(2)}, u32[]{:S(2)}) async-start(bf16[4,128,960]{1,2,0:T(8,128)(2,1)} %bitcast.170), calls=%async_computation.3 | async-start | bytes 1966080 | tf_op jit(solution)/shard_map/all_to_all | solution.py:191
  344.6 32.8 %all-to-all-start.5 = ((bf16[4,240,1280]{2,1,0:T(8,128)(2,1)}), bf16[4,240,1280]{2,1,0:T(8,128)(2,1)}, u32[]{:S(2)}, u32[]{:S(2)}) async-start(bf16[4,240,1280]{2,1,0:T(8,128)(2,1)} %bitcast.178), calls=%async_computation.5 | async-start | bytes 4915200 | tf_op jit(solution)/shard_map/all_to_all | solution.py:307
  390.7 46.5 %all-to-all-start.6 = ((bf16[8,128,640]{2,1,0:T(8,128)(2,1)}), bf16[8,128,640]{2,1,0:T(8,128)(2,1)}, u32[]{:S(2)}, u32[]{:S(2)}) async-start(bf16[8,128,640]{2,1,0:T(8,128)(2,1)} %bitcast.165), calls=%async_computation.6 | async-start | bytes 2621440 | tf_op jit(solution)/shard_map/all_to_all | solution.py:191
  395.1 146.3 %all-reduce.12.cloned.1.call-start = ((), (), s32[]{:S(2)}) async-start(), calls=%async_computation.20 | async-start | bytes 7372800 | tf_op jit(solution)/shard_map/psum | solution.py:320
  398.3 172.3 %reduce-scatter.5.cloned.1.call-start = ((), (), s32[]{:S(2)}) async-start(), calls=%async_computation.17 | async-start | bytes 6144000 | tf_op jit(solution)/shard_map/reduce_scatter | solution.py:185
  401.3 38.0 %copy-start.6 = (f32[128,1280]{1,0:T(8,128)S(1)}, f32[128,1280]{1,0:T(8,128)}, u32[]{:S(2)}) copy-start(f32[128,1280]{1,0:T(8,128)} %copy-done.5) | copy-start | bytes 1966084
  446.5 17.3 %copy-start.81 = (bf16[2,640,960]{1,2,0:T(8,128)(2,1)S(1)}, bf16[2,640,960]{1,2,0:T(8,128)(2,1)}, u32[]{:S(2)}) copy-start(bf16[2,640,960]{1,2,0:T(8,128)(2,1)} %param.21) | copy-start | bytes 7372804
  450.3 13.5 %copy-start.11 = (f32[512,1280]{1,0:T(8,128)S(1)}, f32[512,1280]{1,0:T(8,128)}, u32[]{:S(2)}) copy-start(f32[512,1280]{1,0:T(8,128)} %copy-done.10) | copy-start | bytes 7864324
  470.7 14.4 %all-to-all-start.7 = ((bf16[4,128,960]{1,2,0:T(8,128)(2,1)}), bf16[4,128,960]{1,2,0:T(8,128)(2,1)}, u32[]{:S(2)}, u32[]{:S(2)}) async-start(bf16[4,128,960]{1,2,0:T(8,128)(2,1)} %bitcast.172), calls=%async_computation.7 | async-start | bytes 1966080 | tf_op jit(solution)/shard_map/all_to_all | solution.py:191
  485.1 30.8 %all-to-all-start.8 = ((bf16[4,240,1280]{2,1,0:T(8,128)(2,1)}), bf16[4,240,1280]{2,1,0:T(8,128)(2,1)}, u32[]{:S(2)}, u32[]{:S(2)}) async-start(bf16[4,240,1280]{2,1,0:T(8,128)(2,1)} %bitcast.179), calls=%async_computation.8 | async-start | bytes 4915200 | tf_op jit(solution)/shard_map/all_to_all | solution.py:307
  526.8 46.8 %all-to-all-start.9 = ((bf16[8,128,640]{2,1,0:T(8,128)(2,1)}), bf16[8,128,640]{2,1,0:T(8,128)(2,1)}, u32[]{:S(2)}, u32[]{:S(2)}) async-start(bf16[8,128,640]{2,1,0:T(8,128)(2,1)} %bitcast.164), calls=%async_computation.9 | async-start | bytes 2621440 | tf_op jit(solution)/shard_map/all_to_all | solution.py:191
  541.3 120.7 %all-reduce.10.cloned.1.call-start = ((), (), s32[]{:S(2)}) async-start(), calls=%async_computation.19 | async-start | bytes 7372800 | tf_op jit(solution)/shard_map/psum | solution.py:325
  570.5 153.6 %reduce-scatter.3.cloned.1.call-start = ((), (), s32[]{:S(2)}) async-start(), calls=%async_computation.16 | async-start | bytes 6144000 | tf_op jit(solution)/shard_map/reduce_scatter | solution.py:185
  582.0 211.8 %all-reduce.8.cloned.1.call-start = ((), (), s32[]{:S(2)}) async-start(), calls=%async_computation.18 | async-start | bytes 4915200 | tf_op jit(solution)/shard_map/psum | solution.py:325
  582.1 44.4 %copy-start.68 = (f32[128]{0:T(128)S(1)}, f32[128]{0:T(128)}, u32[]{:S(2)}) copy-start(f32[128]{0:T(128)} %copy-done.66) | copy-start | bytes 1540
  582.1 44.4 %copy-start.76 = (f32[128]{0:T(128)S(1)}, f32[128]{0:T(128)}, u32[]{:S(2)}) copy-start(f32[128]{0:T(128)} %get-tuple-element.201) | copy-start | bytes 1540
  582.1 46.3 %copy-start.29 = (bf16[960,1280]{1,0:T(8,128)(2,1)S(1)}, bf16[960,1280]{1,0:T(8,128)(2,1)}, u32[]{:S(2)}) copy-start(bf16[960,1280]{1,0:T(8,128)(2,1)} %get-tuple-element.53) | copy-start | bytes 7372804
  (72 other events, 203.4 us)
Sparse Core Ops, SparseCore 0:
  14.4 61.3 all-gather.6
  88.2 25.0 all-gather.8
  115.7 89.1 all-gather.10
  253.8 22.8 all-gather.12
  398.7 106.3 all-reduce.11
  508.5 61.9 reduce-scatter.4
  573.0 88.9 all-reduce.9
  665.6 58.4 reduce-scatter.2
  726.6 67.1 all-reduce.7

commit v3 on v2

--- a/solution.py
+++ b/solution.py
@@ -339,7 +339,11 @@
             hidden, attn_gains[l].astype(jnp.float32), grad_normed
         )
         grad = grad_hidden + grad_middle
-        waiting = scatter_sum(jnp.concatenate([grad_qkv, grad_out], axis=1), "fsdp")
+        waiting = jnp.concatenate([grad_qkv, grad_out], axis=1)
+        if l > 0:
+            waiting = scatter_sum(waiting, "fsdp")
+        else:
+            waiting = exchange_sum(waiting, "fsdp").astype(low)
         gain_grads = [(grad_attn_gain, grad_mlp_gain)] + gain_grads
     grad_tokens = grad.astype(low)[None]
     gain_sums = lax.psum(

time: 822 us -> 771 us (0.938)
  waiting for transfers between devices: 358 us -> 262 us
  blocking collectives: 160 us -> 204 us
    reduce_scatter x2 -> x1, waiting for transfers between devices: 91.3 us -> 0.02 us  [scatter_sum(): return lax.psum_scatter(item, axis_name, scatter_dimension=0, tiled=True)]
    psum x1, blocking collectives: 40.3 us -> 84.3 us  [on_device(): lax.psum(jnp.stack([pair[at] for at in (0, 1) for pair in gain_grads]), (...]
    psum x2, waiting for transfers between devices: 90.2 us -> 57.1 us  [on_device(): lax.psum((exchanged, grad_down, attn_grads), 'ctx')]
    all_to_all x5 -> x6, waiting for transfers between devices: 58.8 us -> 87 us  [exchange_sum(): blocks = lax.all_to_all(blocks, axis_name, 0, 0, tiled=True)]
    all_to_all x5 -> x6, starting transfers between devices: 31.7 us -> 35.3 us  [exchange_sum(): blocks = lax.all_to_all(blocks, axis_name, 0, 0, tiled=True)]
    unnamed x191 -> x175, local copies, waits for them, and re-layouts: 36.4 us -> 33.4 us
  transfers between devices with their start and end apart: 18 -> 18, of which waited for: 15 -> 12; matrix products, arithmetic and copies ran while one was open for 14% -> 16% of each run, Pallas kernels for 2% -> 2%
where the time goes in v3:
time: 771 us; the launch traced here: 764 us
  waiting for transfers between devices  262 us (34%)
  blocking collectives  204 us (26%)
  matrix products  73.5 us (10%)
  local copies, waits for them, and re-layouts  70.5 us (9%)
  starting transfers between devices  54.8 us (7%)
  other arithmetic  54.3 us (7%)
  Pallas kernels  28.4 us (4%)
  between operations  15.6 us (2%)
    all_gather x4, blocking collectives, gather(): return lax.all_gather(item, axis_name, axis=0, tiled=True)  97.2 us
    all_to_all x6, waiting for transfers between devices, exchange_sum(): blocks = lax.all_to_all(blocks, axis_name, 0, 0, tiled=True)  87 us
    psum x1, blocking collectives, on_device(): lax.psum(jnp.stack([pair[at] for at in (0, 1) for pair in gain_grads]), (...  84.3 us
    all_gather x4, waiting for transfers between devices, gather(): return lax.all_gather(item, axis_name, axis=0, tiled=True)  61.8 us
    psum x2, waiting for transfers between devices, on_device(): lax.psum((exchanged, grad_down, attn_grads), 'ctx')  57.1 us
    all_to_all x6, starting transfers between devices, exchange_sum(): blocks = lax.all_to_all(blocks, axis_name, 0, 0, tiled=True)  35.3 us
    all_to_all x2, waiting for transfers between devices, on_device(): lax.all_to_all(grad_gate_up.reshape(split, rows, 2 * ff_part), 'fsdp', 0,...  33.8 us
    unnamed x175, local copies, waits for them, and re-layouts  33.4 us
  transfers between devices with their start and end apart: 18, of which 12 were waited for; matrix products, arithmetic and copies ran while one was open for 16% of the time, Pallas kernels for 2%

profile of v3, /device:TPU:0, one launch (start us, length us, event | category | flops | bytes accessed | tf_op | source)
XLA Modules:
  0.0 763.5 jit_solution(16825500640124658124)
XLA Ops:
  15.5 9.5 %all-gather.1 = bf16[4,240,4]{1,2,0:T(4,128)(2,1)S(1)} all-gather(bf16[1,240,4]{1,2,0:T(4,128)(2,1)S(1)} %maximum_bitcast_fusion.8), channel_id=1, replica_groups=mesh['fsdp'=4,'ctx'=8] {'fsdp'}, dimensions={0}, use_global_device_ids=true | all-gather | bytes 9600 | tf_op jit(solution)/shard_map/all_gather | solution.py:228
  26.9 48.9 %all-gather.7.cloned.1.call-done = bf16[960,2560]{1,0:T(8,128)(2,1)} async-done(((bf16[240,2560]{1,0:T(8,128)(2,1)}), bf16[960,2560]{1,0:T(8,128)(2,1)}) %all-gather.7.cloned.1.call-update) | async-done | bytes 4915216 | tf_op jit(solution)/shard_map/all_gather | solution.py:181
  99.6 4.9 all-to-all-start
  116.1 4.3 shard_map.203.mixed_ref
  120.3 21.6 %all-to-all-done = bf16[4,240,1280]{2,1,0:T(8,128)(2,1)} async-done(((bf16[4,240,1280]{2,1,0:T(8,128)(2,1)}), bf16[4,240,1280]{2,1,0:T(8,128)(2,1)}, u32[]{:S(2)}, u32[]{:S(2)}) %all-to-all-start) | async-done | bytes 2457632 | tf_op jit(solution)/shard_map/all_to_all | solution.py:244
  141.9 4.5 all-to-all-start.1
  150.8 57.8 %all_gather.30 = bf16[512,960]{0,1:T(8,128)(2,1)} all-gather(bf16[128,960]{0,1:T(8,128)(2,1)S(1)} %multiply_convert_fusion.8), channel_id=1, replica_groups=mesh['fsdp'=4,'ctx'=8] {'fsdp'}, dimensions={0}, use_global_device_ids=true | all-gather | bytes 1228800 | tf_op jit(solution)/shard_map/all_gather | solution.py:181
  218.9 13.3 %all_to_all.55 = bf16[4,128,960]{1,2,0:T(8,128)(2,1)S(1)} all-to-all(bf16[4,128,960]{1,2,0:T(8,128)(2,1)S(1)} %copy_bitcast_fusion.3), channel_id=1, replica_groups=mesh['fsdp'=4,'ctx'=8] {'fsdp'}, dimensions={0} | all-to-all | bytes 1966080 | tf_op jit(solution)/shard_map/all_to_all | solution.py:191
  253.6 13.0 %all-gather = bf16[1,512,960]{1,2,0:T(8,128)(2,1)} all-gather(bf16[1,128,960]{1,2,0:T(8,128)(2,1)} %param.14), channel_id=2, replica_groups=mesh['fsdp'=4,'ctx'=8] {'fsdp'}, dimensions={1}, use_global_device_ids=true | all-gather | bytes 1228800 | tf_op jit(solution)/shard_map/all_gather | solution.py:181
  267.6 9.1 %all-gather.13.cloned.1.call-done.pair_ref = bf16[1024,640]{1,0:T(8,128)(2,1)} async-done(((bf16[128,640]{1,0:T(8,128)(2,1)}), bf16[1024,640]{1,0:T(8,128)(2,1)}) %all-gather.13.cloned.1.call-update) | async-done | bytes 1310736 | tf_op jit(solution)/shard_map/all_gather | solution.py:181
  278.0 4.3 shard_map.204.mixed_ref
  286.0 13.8 %all_gather.33 = bf16[512,960]{0,1:T(8,128)(2,1)S(1)} all-gather(bf16[128,960]{0,1:T(8,128)(2,1)S(1)} %multiply_convert_fusion.6), channel_id=1, replica_groups=mesh['fsdp'=4,'ctx'=8] {'fsdp'}, dimensions={0}, use_global_device_ids=true | all-gather | bytes 1228800 | tf_op jit(solution)/shard_map/all_gather | solution.py:181
  319.1 8.7 %all-to-all-done.4 = bf16[4,128,960]{1,2,0:T(8,128)(2,1)} async-done(((bf16[4,128,960]{1,2,0:T(8,128)(2,1)}), bf16[4,128,960]{1,2,0:T(8,128)(2,1)}, u32[]{:S(2)}, u32[]{:S(2)}) %all-to-all-start.4) | async-done | bytes 983072 | tf_op jit(solution)/shard_map/all_to_all | solution.py:191
  332.0 4.5 convolution_convert_fusion.3
  336.5 8.0 %all-to-all-done.3 = bf16[4,128,960]{1,2,0:T(8,128)(2,1)} async-done(((bf16[4,128,960]{1,2,0:T(8,128)(2,1)}), bf16[4,128,960]{1,2,0:T(8,128)(2,1)}, u32[]{:S(2)}, u32[]{:S(2)}) %all-to-all-start.3) | async-done | bytes 983072 | tf_op jit(solution)/shard_map/all_to_all | solution.py:191
  344.5 4.7 all-to-all-start.5
  361.4 15.9 %all-to-all-done.5 = bf16[4,240,1280]{2,1,0:T(8,128)(2,1)} async-done(((bf16[4,240,1280]{2,1,0:T(8,128)(2,1)}), bf16[4,240,1280]{2,1,0:T(8,128)(2,1)}, u32[]{:S(2)}, u32[]{:S(2)}) %all-to-all-start.5) | async-done | bytes 2457632 | tf_op jit(solution)/shard_map/all_to_all | solution.py:307
  379.5 10.0 %shard_map.205 = (f32[128,960]{1,0:T(8,128)S(1)}, bf16[1024,640]{1,0:T(8,128)(2,1)S(1)}) custom-call(bf16[128,960]{1,0:T(8,128)(2,1)S(1)} %slice.481.query_ref, bf16[1024,640]{1,0:T(8,128)(2,1)S(1)} %copy-done.3, s32[128,1]{1,0:T(8,128)S(1)} %copy.138.query_place_ref, s32[1,1024]{1,0:T(1,128)S(1)} %bitcast.169, f32[128,960]{1,0:T(8,128)S(1)} %shard_map.204.mixed_ref, ...), custom_call_target="tpu_custom_call" | custom-call | flops 5033164800 | bytes 6000000 | tf_op jit(solution)/shard_map/pallas_call | solution.py:170
  390.6 4.4 all-to-all-start.6
  401.3 34.6 %all-to-all-done.6 = bf16[8,128,640]{2,1,0:T(8,128)(2,1)} async-done(((bf16[8,128,640]{2,1,0:T(8,128)(2,1)}), bf16[8,128,640]{2,1,0:T(8,128)(2,1)}, u32[]{:S(2)}, u32[]{:S(2)}) %all-to-all-start.6) | async-done | bytes 1310752 | tf_op jit(solution)/shard_map/all_to_all | solution.py:191
  443.5 12.7 %all_gather.35 = bf16[512,960]{0,1:T(8,128)(2,1)S(1)} all-gather(bf16[128,960]{0,1:T(8,128)(2,1)S(1)} %get-tuple-element.115), channel_id=1, replica_groups=mesh['fsdp'=4,'ctx'=8] {'fsdp'}, dimensions={0}, use_global_device_ids=true | all-gather | bytes 1228800 | tf_op jit(solution)/shard_map/all_gather | solution.py:181
  477.6 6.0 all-to-all-done.7
  483.6 5.1 all-to-all-start.8
  496.7 17.9 %all-to-all-done.8 = bf16[4,240,1280]{2,1,0:T(8,128)(2,1)} async-done(((bf16[4,240,1280]{2,1,0:T(8,128)(2,1)}), bf16[4,240,1280]{2,1,0:T(8,128)(2,1)}, u32[]{:S(2)}, u32[]{:S(2)}) %all-to-all-start.8) | async-done | bytes 2457632 | tf_op jit(solution)/shard_map/all_to_all | solution.py:307
  514.6 9.8 %shard_map.206 = (f32[128,960]{1,0:T(8,128)S(1)}, bf16[1024,640]{1,0:T(8,128)(2,1)S(1)}) custom-call(bf16[128,960]{1,0:T(8,128)(2,1)S(1)} %slice.449.query_ref, bf16[1024,640]{1,0:T(8,128)(2,1)S(1)} %slice.452.pair_ref, s32[128,1]{1,0:T(8,128)S(1)} %copy.138.query_place_ref, s32[1,1024]{1,0:T(1,128)S(1)} %bitcast.170, f32[128,960]{1,0:T(8,128)S(1)} %shard_map.203.mixed_ref, ...), custom_call_target="tpu_custom_call" | custom-call | flops 5033164800 | bytes 6000000 | tf_op jit(solution)/shard_map/pallas_call | solution.py:170
  525.5 13.2 %all-to-all-start.9 = ((bf16[8,128,640]{2,1,0:T(8,128)(2,1)}), bf16[8,128,640]{2,1,0:T(8,128)(2,1)}, u32[]{:S(2)}, u32[]{:S(2)}) async-start(bf16[8,128,640]{2,1,0:T(8,128)(2,1)} %bitcast.166), calls=%async_computation.9 | async-start | bytes 2621440 | tf_op jit(solution)/shard_map/all_to_all | solution.py:191
  541.3 29.7 %all-to-all-done.9 = bf16[8,128,640]{2,1,0:T(8,128)(2,1)} async-done(((bf16[8,128,640]{2,1,0:T(8,128)(2,1)}), bf16[8,128,640]{2,1,0:T(8,128)(2,1)}, u32[]{:S(2)}, u32[]{:S(2)}) %all-to-all-start.9) | async-done | bytes 1310752 | tf_op jit(solution)/shard_map/all_to_all | solution.py:191
  579.0 5.0 all-to-all-start.10
  588.1 84.3 %psum.49 = f32[4,960]{1,0:T(4,128)S(1)} all-reduce(f32[4,960]{1,0:T(4,128)S(1)} %pad_maximum_fusion.21), channel_id=1, replica_groups=mesh['fsdp'=4,'ctx'=8] {'fsdp','ctx'}, use_global_device_ids=true, to_apply=%region_19.20 | all-reduce | flops 3840 | bytes 30720 | tf_op jit(solution)/shard_map/psum | solution.py:349
  673.4 4.7 reduce_sum.204
  681.1 4.3 maximum_convert_fusion.2
  691.1 57.1 %all-reduce.8.cloned.1.call-done = (bf16[240,2560]{1,0:T(8,128)(2,1)}, bf16[240,2560]{1,0:T(8,128)(2,1)}) async-done(((bf16[240,2560]{1,0:T(8,128)(2,1)}, bf16[240,2560]{1,0:T(8,128)(2,1)}), (bf16[240,2560]{1,0:T(8,128)(2,1)}, bf16[240,2560]{1,0:T(8,128)(2,1)})) %all-reduce.8.cloned.1.call-update) | async-done | bytes 2457616 | tf_op jit(solution)/shard_map/psum | solution.py:325
  (337 shorter events, 202.5 us)
Async XLA Ops:
  7.2 68.6 %all-gather.7.cloned.1.call-start = ((), (), s32[]{:S(2)}) async-start(), calls=%async_computation.12 | async-start | bytes 6144000 | tf_op jit(solution)/shard_map/all_gather | solution.py:181
  14.2 11.3 %copy-start.24 = (bf16[1,128,960]{1,2,0:T(8,128)(2,1)S(1)}, bf16[1,128,960]{1,2,0:T(8,128)(2,1)}, u32[]{:S(2)}) copy-start(bf16[1,128,960]{1,2,0:T(8,128)(2,1)} %param.12) | copy-start | bytes 737284
  14.3 99.0 %all-gather.9.cloned.1.call-start = ((), (), s32[]{:S(2)}) async-start(), calls=%async_computation.13 | async-start | bytes 1769472 | tf_op jit(solution)/shard_map/all_gather | solution.py:181
  15.4 69.8 %copy-start.16 = (f32[128,1280]{1,0:T(8,128)}, f32[128,1280]{1,0:T(8,128)S(1)}, u32[]{:S(2)}) copy-start(f32[128,1280]{1,0:T(8,128)S(1)} %copy.135) | copy-start | bytes 1966084
  25.4 224.7 %copy-start.5 = (f32[128,1280]{1,0:T(8,128)}, f32[128,1280]{1,0:T(8,128)S(1)}, u32[]{:S(2)}) copy-start(f32[128,1280]{1,0:T(8,128)S(1)} %copy.130) | copy-start | bytes 1966084
  26.3 53.0 %copy-start.60 = (f32[128]{0:T(128)}, f32[128]{0:T(128)S(1)}, u32[]{:S(2)}) copy-start(f32[128]{0:T(128)S(1)} %get-tuple-element.202) | copy-start | bytes 1540
  26.9 52.4 %copy-start.52 = (f32[1,960]{1,0:T(1,128)}, f32[1,960]{1,0:T(1,128)S(1)}, u32[]{:S(2)}) copy-start(f32[1,960]{1,0:T(1,128)S(1)} %get-tuple-element.195) | copy-start | bytes 11524
  88.1 120.5 %all-gather.11.cloned.1.call-start = ((), (), s32[]{:S(2)}) async-start(), calls=%async_computation.14 | async-start | bytes 6144000 | tf_op jit(solution)/shard_map/all_gather | solution.py:181
  99.6 42.3 %all-to-all-start = ((bf16[4,240,1280]{2,1,0:T(8,128)(2,1)}), bf16[4,240,1280]{2,1,0:T(8,128)(2,1)}, u32[]{:S(2)}, u32[]{:S(2)}) async-start(bf16[4,240,1280]{2,1,0:T(8,128)(2,1)} %pad_maximum_fusion.2), calls=%async_computation | async-start | bytes 4915200 | tf_op jit(solution)/shard_map/all_to_all | solution.py:244
  141.9 75.6 %all-to-all-start.1 = ((bf16[4,240,1280]{2,1,0:T(8,128)(2,1)}), bf16[4,240,1280]{2,1,0:T(8,128)(2,1)}, u32[]{:S(2)}, u32[]{:S(2)}) async-start(bf16[4,240,1280]{2,1,0:T(8,128)(2,1)} %pad_maximum_fusion.3), calls=%async_computation.1 | async-start | bytes 4915200 | tf_op jit(solution)/shard_map/all_to_all | solution.py:244
  146.5 130.2 %all-gather.13.cloned.1.call-start = ((), (), s32[]{:S(2)}) async-start(), calls=%async_computation.15 | async-start | bytes 1474560 | tf_op jit(solution)/shard_map/all_gather | solution.py:181
  150.1 82.2 %copy-start.8 = (f32[128,960]{0,1:T(8,128)}, f32[128,960]{0,1:T(8,128)S(1)}, u32[]{:S(2)}) copy-start(f32[128,960]{0,1:T(8,128)S(1)} %get-tuple-element.212) | copy-start | bytes 1474564
  150.6 61.5 %copy-start.57 = (f32[128]{0:T(128)}, f32[128]{0:T(128)S(1)}, u32[]{:S(2)}) copy-start(f32[128]{0:T(128)S(1)} %get-tuple-element.204) | copy-start | bytes 1540
  218.9 14.1 %copy-start.54 = (f32[1,960]{1,0:T(1,128)S(1)}, f32[1,960]{1,0:T(1,128)}, u32[]{:S(2)}) copy-start(f32[1,960]{1,0:T(1,128)} %get-tuple-element.193) | copy-start | bytes 11524
  311.3 16.5 %all-to-all-start.4 = ((bf16[4,128,960]{1,2,0:T(8,128)(2,1)}), bf16[4,128,960]{1,2,0:T(8,128)(2,1)}, u32[]{:S(2)}, u32[]{:S(2)}) async-start(bf16[4,128,960]{1,2,0:T(8,128)(2,1)} %bitcast.173), calls=%async_computation.4 | async-start | bytes 1966080 | tf_op jit(solution)/shard_map/all_to_all | solution.py:191
  327.8 16.7 %all-to-all-start.3 = ((bf16[4,128,960]{1,2,0:T(8,128)(2,1)}), bf16[4,128,960]{1,2,0:T(8,128)(2,1)}, u32[]{:S(2)}, u32[]{:S(2)}) async-start(bf16[4,128,960]{1,2,0:T(8,128)(2,1)} %bitcast.172), calls=%async_computation.3 | async-start | bytes 1966080 | tf_op jit(solution)/shard_map/all_to_all | solution.py:191
  344.5 32.8 %all-to-all-start.5 = ((bf16[4,240,1280]{2,1,0:T(8,128)(2,1)}), bf16[4,240,1280]{2,1,0:T(8,128)(2,1)}, u32[]{:S(2)}, u32[]{:S(2)}) async-start(bf16[4,240,1280]{2,1,0:T(8,128)(2,1)} %bitcast.180), calls=%async_computation.5 | async-start | bytes 4915200 | tf_op jit(solution)/shard_map/all_to_all | solution.py:307
  390.6 45.3 %all-to-all-start.6 = ((bf16[8,128,640]{2,1,0:T(8,128)(2,1)}), bf16[8,128,640]{2,1,0:T(8,128)(2,1)}, u32[]{:S(2)}, u32[]{:S(2)}) async-start(bf16[8,128,640]{2,1,0:T(8,128)(2,1)} %bitcast.165), calls=%async_computation.6 | async-start | bytes 2621440 | tf_op jit(solution)/shard_map/all_to_all | solution.py:191
  395.0 189.1 %all-reduce.12.cloned.1.call-start = ((), (), s32[]{:S(2)}) async-start(), calls=%async_computation.19 | async-start | bytes 7372800 | tf_op jit(solution)/shard_map/psum | solution.py:320
  401.2 36.8 %copy-start.6 = (f32[128,1280]{1,0:T(8,128)S(1)}, f32[128,1280]{1,0:T(8,128)}, u32[]{:S(2)}) copy-start(f32[128,1280]{1,0:T(8,128)} %copy-done.5) | copy-start | bytes 1966084
  401.2 182.9 %reduce-scatter.2.cloned.1.call-start = ((), (), s32[]{:S(2)}) async-start(), calls=%async_computation.16 | async-start | bytes 6144000 | tf_op jit(solution)/shard_map/reduce_scatter | solution.py:185
  443.5 13.8 %copy-start.11 = (bf16[960,960]{1,0:T(8,128)(2,1)S(1)}, bf16[960,960]{1,0:T(8,128)(2,1)}, u32[]{:S(2)}) copy-start(bf16[960,960]{1,0:T(8,128)(2,1)} %convolution_convert_fusion.4) | copy-start | bytes 5529604
  469.2 14.4 %all-to-all-start.7 = ((bf16[4,128,960]{1,2,0:T(8,128)(2,1)}), bf16[4,128,960]{1,2,0:T(8,128)(2,1)}, u32[]{:S(2)}, u32[]{:S(2)}) async-start(bf16[4,128,960]{1,2,0:T(8,128)(2,1)} %bitcast.174), calls=%async_computation.7 | async-start | bytes 1966080 | tf_op jit(solution)/shard_map/all_to_all | solution.py:191
  483.6 31.0 %all-to-all-start.8 = ((bf16[4,240,1280]{2,1,0:T(8,128)(2,1)}), bf16[4,240,1280]{2,1,0:T(8,128)(2,1)}, u32[]{:S(2)}, u32[]{:S(2)}) async-start(bf16[4,240,1280]{2,1,0:T(8,128)(2,1)} %bitcast.181), calls=%async_computation.8 | async-start | bytes 4915200 | tf_op jit(solution)/shard_map/all_to_all | solution.py:307
  525.5 45.6 %all-to-all-start.9 = ((bf16[8,128,640]{2,1,0:T(8,128)(2,1)}), bf16[8,128,640]{2,1,0:T(8,128)(2,1)}, u32[]{:S(2)}, u32[]{:S(2)}) async-start(bf16[8,128,640]{2,1,0:T(8,128)(2,1)} %bitcast.166), calls=%async_computation.9 | async-start | bytes 2621440 | tf_op jit(solution)/shard_map/all_to_all | solution.py:191
  540.7 32.4 %copy-start.7 = (f32[128,1280]{1,0:T(8,128)S(1)}, f32[128,1280]{1,0:T(8,128)}, u32[]{:S(2)}) copy-start(f32[128,1280]{1,0:T(8,128)} %copy-done.5) | copy-start | bytes 1966084
  540.7 32.4 %copy-start.19 = (f32[128,1280]{1,0:T(8,128)S(1)}, f32[128,1280]{1,0:T(8,128)}, u32[]{:S(2)}) copy-start(f32[128,1280]{1,0:T(8,128)} %copy.156) | copy-start | bytes 1966084
  579.0 94.4 %all-to-all-start.10 = ((bf16[4,240,2560]{2,1,0:T(8,128)(2,1)}), bf16[4,240,2560]{2,1,0:T(8,128)(2,1)}, u32[]{:S(2)}, u32[]{:S(2)}) async-start(bf16[4,240,2560]{2,1,0:T(8,128)(2,1)} %bitcast.171), calls=%async_computation.10 | async-start | bytes 9830400 | tf_op jit(solution)/shard_map/all_to_all | solution.py:191
  584.0 95.2 %all-reduce.10.cloned.1.call-start = ((), (), s32[]{:S(2)}) async-start(), calls=%async_computation.18 | async-start | bytes 7372800 | tf_op jit(solution)/shard_map/psum | solution.py:325
  584.8 163.5 %all-reduce.8.cloned.1.call-start = ((), (), s32[]{:S(2)}) async-start(), calls=%async_computation.17 | async-start | bytes 4915200 | tf_op jit(solution)/shard_map/psum | solution.py:325
  585.0 87.5 %copy-start.62 = (f32[128]{0:T(128)S(1)}, f32[128]{0:T(128)}, u32[]{:S(2)}) copy-start(f32[128]{0:T(128)} %copy-done.60) | copy-start | bytes 1540
  585.0 87.5 %copy-start.69 = (f32[128]{0:T(128)S(1)}, f32[128]{0:T(128)}, u32[]{:S(2)}) copy-start(f32[128]{0:T(128)} %get-tuple-element.201) | copy-start | bytes 1540
  (64 other events, 199.4 us)
Sparse Core Ops, SparseCore 0:
  14.4 61.3 all-gather.6
  88.2 25.0 all-gather.8
  115.7 89.1 all-gather.10
  253.7 22.8 all-gather.12
  401.3 103.5 all-reduce.11
  508.4 60.6 reduce-scatter.1
  587.3 88.3 all-reduce.9
  681.2 67.0 all-reduce.7
